TPU v7x, 256 devices: a whole 4x4x8 slice. The times are simulated.
256 devices in a mesh: dp: 4 (over z_hi, core), ctx: 64 (over y, z_lo, x).
Axes of the slice: x: 4, y: 4, z: 8 (z_hi: 2, z_lo: 4; z = z_hi * 4 + z_lo), core: 2. Of those that a mesh axis runs over, the one named last changes fastest.
Arguments:
- query_in: bfloat16 [4, 8192, 512], P('dp', 'ctx'), may hold values from -6 to 6
- key_in: bfloat16 [4, 8192, 512], P('dp', 'ctx'), may hold values from -6 to 6
- value_in: bfloat16 [4, 8192, 512], P('dp', 'ctx'), may hold values from -6 to 6
- short_taps: float32 [3, 3, 512], replicated, may hold values from -3 to 3
- long_filter: float32 [8192, 512], P('ctx'), may hold values from -6 to 6
- cotangent: bfloat16 [4, 8192, 512], P('dp', 'ctx'), may hold values from -6 to 6
Outputs:
- grad_query: bfloat16 [4, 8192, 512], P('dp', 'ctx')
- grad_key: bfloat16 [4, 8192, 512], P('dp', 'ctx')
- grad_value: bfloat16 [4, 8192, 512], P('dp', 'ctx')
- grad_taps: float32 [3, 3, 512], replicated
- grad_filter: float32 [8192, 512], P('ctx')
All inputs are finite; a program needn't handle non-finite values.
Results may differ from a plain program's by a relative error of at most 0.014.
Values may be sent and summed in bfloat16 or wider, within the bound.
A program may use at most 64 MiB of HBM per device.

v0:
```python
import functools
import math

import jax
import jax.numpy as jnp
import numpy as np
from jax import lax
from jax.experimental import pallas as pl
from jax.experimental.pallas import tpu as pltpu
from jax.sharding import PartitionSpec as P

MESH = pl.DeviceIdType.MESH
F32 = jnp.float32
BF16 = jnp.bfloat16

NZ, NPLANE, NCTX = 8, 16, 64
GROUP = NZ * NPLANE
CHAN = 4
SEQ = 2
POS = 128
ROWS = 16


def split_np(table):
    high = table.astype(jnp.bfloat16)
    low = (table - high.astype(np.float64)).astype(jnp.bfloat16)
    return high, low


@functools.cache
def tables():
    length = NCTX * POS
    a = np.arange(NCTX, dtype=np.float64)
    b = np.arange(POS, dtype=np.float64)
    outer = 2 * np.pi * np.outer(a, a + 0.25) / NCTX
    turn = 2 * np.pi * np.outer(a + 0.25, b) / length
    inner = 2 * np.pi * (np.outer(b, b) % POS) / POS
    first = np.concatenate([np.cos(outer.T), -np.sin(outer.T)], axis=0)
    high, low = split_np(first)
    first_cat = np.concatenate([high, low, high], axis=1)
    scale = 1.0 / (length * math.sqrt(length))
    last = np.concatenate([np.cos(outer), -np.sin(outer)], axis=1) * scale
    high, low = split_np(last)
    last_cat = np.concatenate([high, low, high], axis=1)
    c, s = np.cos(inner), np.sin(inner)
    forward = np.stack(split_np(np.block([[c, -s], [s, c]])))
    inverse = np.stack(split_np(np.block([[c, s], [-s, c]])))
    twiddle = np.stack([np.cos(turn), np.sin(turn)]).astype(np.float32)
    pick = np.zeros((32, 4, CHAN, 4, POS), np.float32)
    for g in range(32):
        for f in range(4):
            for i in range(CHAN):
                pick[g, f, i, f, CHAN * g + i] = 1
    pick = pick.reshape(512, 512).astype(jnp.bfloat16)
    pick_one = np.zeros((32, 8, POS), np.float32)
    for g in range(32):
        for i in range(CHAN):
            pick_one[g, i, CHAN * g + i] = 1
    pick_one = pick_one.reshape(256, POS).astype(jnp.bfloat16)
    return first_cat, last_cat, forward, inverse, twiddle, pick, pick_one


def split(x):
    high = x.astype(BF16)
    return high, (x - high.astype(F32)).astype(BF16)


def dot(a, b):
    return jnp.dot(a, b, preferred_element_type=F32)


def dot_nt(a, b):
    return lax.dot_general(a, b, (((1,), (1,)), ((), ())), preferred_element_type=F32)


def stack_split(x):
    high, low = split(x)
    return jnp.concatenate([high, high, low], axis=0)


def wide_dot(x, table):
    high, low = split(x)
    return dot(high, table[0]) + (dot(high, table[1]) + dot(low, table[0]))


def kernel(
    q_ref, k_ref, v_ref, c_ref, filt_ref, taps_ref,
    first_ref, last_ref, fwd_ref, inv_ref, tw_ref, pick_ref, pick1_ref,
    gq_ref, gk_ref, gv_ref, gt_ref, gf_ref,
    send_buf, recv_buf, fsend, frecv, raw, fraw, spec, hspec, keep, pack, rsend, rrecv,
    corr_buf, sib_send, sib_recv, tap_rows, tap_own, tap_sib, tap_send, tap_recv,
    send_sem, recv_sem, fsend_sem, frecv_sem, rsend_sem, rrecv_sem,
    sib_sems, tap_sems, plane_sem,
):
    dp, cx = lax.axis_index("dp"), lax.axis_index("ctx")
    zh, core = dp // 2, lax.rem(dp, 2)
    y, zl, x = cx // 16, lax.rem(cx // 4, 4), lax.rem(cx, 4)
    z = zh * 4 + zl
    me = zh * NCTX + cx

    def place(zt, yt, xt, core_t):
        half = zt // 4
        ctx = yt * 16 + lax.rem(zt, 4) * 4 + xt
        return (half * 2 + core_t, ctx), half * NCTX + ctx

    def in_plane(zt, r):
        return place(zt, lax.rem(y + r // 4, 4), lax.rem(x + lax.rem(r, 4), 4), core)

    def plane_of(k):
        return lax.rem(z + k, NZ)

    sibling = (zh * 2 + (1 - core), cx)

    barrier = pltpu.get_barrier_semaphore()

    def greet(r, carry):
        pl.semaphore_signal(barrier, inc=1, device_id=in_plane(z, r)[0], device_id_type=MESH)
        return carry

    lax.fori_loop(1, NPLANE, greet, 0)
    for k in range(1, NZ):
        pl.semaphore_signal(barrier, inc=1, device_id=place(plane_of(k), y, x, core)[0], device_id_type=MESH)
    pl.semaphore_signal(barrier, inc=1, device_id=sibling, device_id_type=MESH)

    for j in range(4):
        lanes = slice(j * POS, (j + 1) * POS)
        fields = jnp.concatenate([q_ref[:, lanes], k_ref[:, lanes], v_ref[:, lanes], c_ref[:, lanes]], axis=1)
        rows = dot_nt(pick_ref[...], fields).astype(BF16)
        send_buf[pl.ds(j * 32, 32)] = rows.reshape(32, ROWS, POS)
        high, low = split(filt_ref[:, lanes])
        rows = dot_nt(pick1_ref[...], high) + dot_nt(pick1_ref[...], low)
        fsend[pl.ds(j * 32, 32)] = rows.reshape(32, 8, POS)[:, :CHAN, :]

    pl.semaphore_wait(barrier, NPLANE - 1 + NZ - 1 + 1)
    for k in range(1, NZ):
        pl.semaphore_signal(
            plane_sem.at[NZ - k], inc=1, device_id=place(plane_of(k), y, x, core)[0], device_id_type=MESH
        )

    near = (0, 1, 2, 7)
    own = pltpu.make_async_copy(send_buf.at[me], recv_buf.at[me], recv_sem.at[zh])
    own.start()
    fown = pltpu.make_async_copy(fsend.at[me], frecv.at[cx], frecv_sem)
    fown.start()
    for k in (0, 7, 1, 6, 2, 5, 3, 4):
        if k:
            pl.semaphore_wait(plane_sem.at[k], 1)

        def send(r, carry, k=k):
            to, owner = in_plane(plane_of(k), r)
            if k in near:
                pltpu.make_async_remote_copy(
                    src_ref=fsend.at[owner], dst_ref=frecv.at[cx], send_sem=fsend_sem, recv_sem=frecv_sem,
                    device_id=to, device_id_type=MESH,
                ).start()
            pltpu.make_async_remote_copy(
                src_ref=send_buf.at[owner], dst_ref=recv_buf.at[me], send_sem=send_sem, recv_sem=recv_sem.at[zh],
                device_id=to, device_id_type=MESH,
            ).start()
            return carry

        lax.fori_loop(0 if k else 1, NPLANE, send, 0)

    def wait_bytes(ref, sem):
        pltpu.make_async_copy(ref, ref, sem).wait()

    row_id = lax.broadcasted_iota(jnp.int32, (NCTX, POS), 0)
    lane_id = lax.broadcasted_iota(jnp.int32, (NCTX, POS), 1)

    def before(v, s):
        turned = pltpu.roll(v, s, 1)
        carried = jnp.where(row_id == 0, 0.0, pltpu.roll(turned, 1, 0))
        return jnp.where(lane_id < s, carried, turned)

    def after(v, s):
        turned = pltpu.roll(v, POS - s, 1)
        carried = jnp.where(row_id == NCTX - 1, 0.0, pltpu.roll(turned, NCTX - 1, 0))
        return jnp.where(lane_id >= POS - s, carried, turned)

    def tap(branch, j, i):
        return taps_ref[branch * 3 + j, me * CHAN + i]

    def field(h, f, i):
        return raw[pl.ds(h * NCTX * ROWS + f * CHAN + i, NCTX, ROWS), :]

    cos, sin = tw_ref[0], tw_ref[1]

    def spectrum(values):
        turned = dot(first_ref[...], stack_split(jnp.concatenate(values, axis=1)))
        parts = []
        for n in range(len(values)):
            re, im = turned[:NCTX, n * POS:(n + 1) * POS], turned[NCTX:, n * POS:(n + 1) * POS]
            parts.append(jnp.concatenate([re * cos + im * sin, im * cos - re * sin], axis=1))
        return wide_dot(jnp.concatenate(parts, axis=0), fwd_ref)

    def signal(spectra):
        joined = jnp.concatenate([jnp.concatenate(s, axis=1) for s in spectra], axis=0)
        turned = wide_dot(joined, inv_ref)
        parts = []
        for n in range(len(spectra)):
            re, im = turned[n * NCTX:(n + 1) * NCTX, :POS], turned[n * NCTX:(n + 1) * NCTX, POS:]
            parts.append(jnp.concatenate([re * cos - im * sin, re * sin + im * cos], axis=0))
        return dot(last_ref[...], stack_split(jnp.concatenate(parts, axis=1)))

    def halves(ref, n):
        return ref[n * NCTX:(n + 1) * NCTX, :POS], ref[n * NCTX:(n + 1) * NCTX, POS:]

    wait_bytes(frecv, frecv_sem)
    filt = frecv[...]
    fraw[...] = jnp.concatenate([filt, jnp.zeros_like(filt)], axis=1).reshape(NCTX * 8, POS)
    hspec[...] = spectrum([fraw[pl.ds(i, NCTX, 8), :] for i in range(CHAN)])

    for h in range(SEQ):
        wait_bytes(recv_buf.at[pl.ds(h * NCTX, NCTX)], recv_sem.at[h])
        raw[pl.ds(h * NCTX * ROWS, NCTX * ROWS), :] = (
            recv_buf[pl.ds(h * NCTX, NCTX)].astype(F32).reshape(NCTX * ROWS, POS)
        )
        values = []
        for i in range(CHAN):
            feats = []
            for branch in range(3):
                v = field(h, branch, i)
                feats.append(
                    tap(branch, 0, i) * v + tap(branch, 1, i) * before(v, 1) + tap(branch, 2, i) * before(v, 2)
                )
            keep[h, i, 0] = feats[1]
            keep[h, i, 1] = feats[2]
            values += [feats[1] * feats[2], feats[0] * field(h, 3, i)]
        spec[h] = spectrum(values)

    corrs = []
    for i in range(CHAN):
        re = im = 0.0
        for h in range(SEQ):
            mr, mi = halves(spec.at[h], 2 * i)
            gr, gi = halves(spec.at[h], 2 * i + 1)
            re, im = re + (mr * gr + mi * gi), im + (mr * gi - mi * gr)
        corrs.append((re, im))
    sib_send[...] = signal(corrs)
    sib = pltpu.make_async_remote_copy(
        src_ref=sib_send, dst_ref=sib_recv, send_sem=sib_sems.at[0], recv_sem=sib_sems.at[1],
        device_id=sibling, device_id_type=MESH,
    )
    sib.start()

    tap_rows[...] = jnp.zeros_like(tap_rows)
    for h in range(SEQ):
        spectra = []
        for i in range(CHAN):
            fr, fi = halves(hspec, i)
            mr, mi = halves(spec.at[h], 2 * i)
            gr, gi = halves(spec.at[h], 2 * i + 1)
            spectra += [(fr * mr - fi * mi, fr * mi + fi * mr), (fr * gr + fi * gi, fr * gi - fi * gr)]
        back = signal(spectra)
        for i in range(CHAN):
            conv = back[:, 2 * i * POS:(2 * i + 1) * POS]
            adj = back[:, (2 * i + 1) * POS:(2 * i + 2) * POS]
            grads = [field(h, 3, i) * conv, adj * keep[h, i, 1], adj * keep[h, i, 0]]
            for branch in range(3):
                d, v = grads[branch], field(h, branch, i)
                pack[pl.ds(h * NCTX * ROWS + branch * CHAN + i, NCTX, ROWS), :] = (
                    tap(branch, 0, i) * d + tap(branch, 1, i) * after(d, 1) + tap(branch, 2, i) * after(d, 2)
                )
                for j in range(3):
                    term = d * (before(v, j) if j else v)
                    row = (branch * 3 + j) * CHAN + i
                    tap_rows[row:row + 1, :] += jnp.sum(term, axis=0, keepdims=True)

    ones = jnp.ones((8, POS), F32)
    scale = 1.0 / math.sqrt(SEQ * 2 * NCTX * POS)
    sums = lax.dot_general(
        ones, tap_rows[...], (((1,), (1,)), ((), ())), precision=lax.Precision.HIGHEST, preferred_element_type=F32
    )
    tap_own[...] = sums[0:1] * scale
    tap_sibling = pltpu.make_async_remote_copy(
        src_ref=tap_own, dst_ref=tap_sib, send_sem=tap_sems.at[0], recv_sem=tap_sems.at[1],
        device_id=sibling, device_id_type=MESH,
    )
    tap_sibling.start()

    sib.wait_recv()
    for i in range(CHAN):
        total = sib_send[:, i * POS:(i + 1) * POS] + sib_recv[:, i * POS:(i + 1) * POS]
        for h in range(SEQ):
            pack[pl.ds(h * NCTX * ROWS + 3 * CHAN + i, NCTX, ROWS), :] = total
    rsend[...] = pack[...].reshape(GROUP, ROWS, POS).astype(BF16)

    rown = pltpu.make_async_copy(rsend.at[me], rrecv.at[me], rrecv_sem)
    rown.start()
    for k in (0, 7, 1, 6, 2, 5, 3, 4):
        def give(r, carry, k=k):
            to, owner = in_plane(plane_of(k), r)
            pltpu.make_async_remote_copy(
                src_ref=rsend.at[owner], dst_ref=rrecv.at[me], send_sem=rsend_sem, recv_sem=rrecv_sem,
                device_id=to, device_id_type=MESH,
            ).start()
            return carry

        lax.fori_loop(0 if k else 1, NPLANE, give, 0)

    tap_sibling.wait_recv()
    tap_send[...] = tap_own[...] + tap_sib[...]
    town = pltpu.make_async_copy(tap_send, tap_recv.at[me], tap_sems.at[3])
    town.start()
    for k in (0, 7, 1, 6, 2, 5, 3, 4):
        def tell(r, carry, k=k):
            to, owner = in_plane(plane_of(k), r)
            pltpu.make_async_remote_copy(
                src_ref=tap_send, dst_ref=tap_recv.at[me], send_sem=tap_sems.at[2], recv_sem=tap_sems.at[3],
                device_id=to, device_id_type=MESH,
            ).start()
            return carry

        lax.fori_loop(0 if k else 1, NPLANE, tell, 0)

    wait_bytes(send_buf.at[pl.ds(0, GROUP - 1)], send_sem)
    wait_bytes(fsend.at[pl.ds(0, NCTX - 1)], fsend_sem)
    sib.wait_send()
    tap_sibling.wait_send()

    wait_bytes(tap_recv, tap_sems.at[3])
    taps_all = tap_recv[...].reshape(GROUP, POS)
    total = jnp.zeros((16, GROUP * CHAN), F32)
    for i in range(CHAN):
        pick_row = (
            lax.broadcasted_iota(jnp.int32, (16, POS), 1)
            == CHAN * lax.broadcasted_iota(jnp.int32, (16, POS), 0) + i
        ).astype(F32)
        spread = (
            lax.broadcasted_iota(jnp.int32, (GROUP, GROUP * CHAN), 1)
            == CHAN * lax.broadcasted_iota(jnp.int32, (GROUP, GROUP * CHAN), 0) + i
        ).astype(F32)
        rows = lax.dot_general(
            pick_row, taps_all, (((1,), (1,)), ((), ())),
            precision=lax.Precision.HIGHEST, preferred_element_type=F32,
        )
        total += jnp.dot(rows, spread, precision=lax.Precision.HIGHEST, preferred_element_type=F32)
    gt_ref[...] = total

    wait_bytes(rrecv, rrecv_sem)
    for j in range(4):
        lanes = slice(j * POS, (j + 1) * POS)
        rows = rrecv[pl.ds(j * 32, 32)].reshape(512, POS)
        out = lax.dot_general(rows, pick_ref[...], (((0,), (0,)), ((), ())), preferred_element_type=F32)
        gq_ref[:, lanes] = out[:, :POS].astype(BF16)
        gk_ref[:, lanes] = out[:, POS:2 * POS].astype(BF16)
        gv_ref[:, lanes] = out[:, 2 * POS:3 * POS].astype(BF16)
        gf_ref[:, lanes] = out[:, 3 * POS:]
    wait_bytes(rsend.at[pl.ds(0, GROUP - 1)], rsend_sem)
    for _ in range(1):
        wait_bytes(tap_recv.at[pl.ds(0, GROUP - 1)], tap_sems.at[2])


def per_device(query_in, key_in, value_in, short_taps, long_filter, cotangent):
    rows, channels = query_in.shape[1:]
    vmem = pl.BlockSpec(memory_space=pltpu.VMEM)
    shape = jax.ShapeDtypeStruct
    scratch = [
        pltpu.VMEM((GROUP, ROWS, POS), BF16),
        pltpu.VMEM((GROUP, ROWS, POS), BF16),
        pltpu.VMEM((GROUP, CHAN, POS), F32),
        pltpu.VMEM((NCTX, CHAN, POS), F32),
        pltpu.VMEM((GROUP * ROWS, POS), F32),
        pltpu.VMEM((NCTX * 8, POS), F32),
        pltpu.VMEM((SEQ, 2 * CHAN * NCTX, 2 * POS), F32),
        pltpu.VMEM((CHAN * NCTX, 2 * POS), F32),
        pltpu.VMEM((SEQ, CHAN, 2, NCTX, POS), F32),
        pltpu.VMEM((GROUP * ROWS, POS), F32),
        pltpu.VMEM((GROUP, ROWS, POS), BF16),
        pltpu.VMEM((GROUP, ROWS, POS), BF16),
        pltpu.VMEM((8, POS), F32),
        pltpu.VMEM((NCTX, CHAN * POS), F32),
        pltpu.VMEM((NCTX, CHAN * POS), F32),
        pltpu.VMEM((POS, POS), F32),
        pltpu.VMEM((1, POS), F32),
        pltpu.VMEM((1, POS), F32),
        pltpu.VMEM((1, POS), F32),
        pltpu.VMEM((GROUP, 1, POS), F32),
        pltpu.SemaphoreType.DMA,
        pltpu.SemaphoreType.DMA((SEQ,)),
        pltpu.SemaphoreType.DMA,
        pltpu.SemaphoreType.DMA,
        pltpu.SemaphoreType.DMA,
        pltpu.SemaphoreType.DMA,
        pltpu.SemaphoreType.DMA((2,)),
        pltpu.SemaphoreType.DMA((4,)),
        pltpu.SemaphoreType.REGULAR((NZ,)),
    ]
    outs = pl.pallas_call(
        kernel,
        out_shape=(
            shape((rows, channels), BF16),
            shape((rows, channels), BF16),
            shape((rows, channels), BF16),
            shape((16, channels), F32),
            shape((rows, channels), F32),
        ),
        in_specs=[vmem] * 5 + [pl.BlockSpec(memory_space=pltpu.SMEM)] + [vmem] * 7,
        out_specs=[vmem] * 5,
        scratch_shapes=scratch,
        compiler_params=pltpu.CompilerParams(
            collective_id=0, has_side_effects=True, vmem_limit_bytes=48 * 1024 * 1024
        ),
    )(
        query_in[0], key_in[0], value_in[0], cotangent[0], long_filter,
        short_taps.reshape(9, channels), *(jnp.asarray(t) for t in tables()),
    )
    grad_query, grad_key, grad_value, grad_taps, grad_filter = outs
    return (
        grad_query[None], grad_key[None], grad_value[None],
        grad_taps[:9].reshape(short_taps.shape), grad_filter,
    )


def solution(mesh):
    seq = P("dp", "ctx", None)
    return jax.shard_map(
        per_device,
        mesh=mesh,
        in_specs=(seq, seq, seq, P(), P("ctx", None), seq),
        out_specs=(seq, seq, seq, P(), P("ctx", None)),
        check_vma=False,
    )
```

profile of v0, /device:TPU:1, one launch (start us, length us, event | category | flops | bytes accessed | tf_op | source)
XLA Modules:
  0.0 69.4 jit_solution(5062231318074637539)
XLA Ops:
  0.6 0.0 copy-start.8
  0.6 0.8 %reshape.16.taps_ref = f32[9,512]{1,0:T(8,128)S(1)} reshape(f32[3,3,512]{2,1,0:T(4,128)} %param.16) | data formatting | bytes 36864 | tf_op jit(solution)/shard_map/reshape | solution.py:406
  1.4 0.0 copy-done.8
  1.5 0.0 copy-start
  1.5 1.0 %copy-done = bf16[512,512]{1,0:T(8,128)(2,1)S(1)} copy-done((bf16[512,512]{1,0:T(8,128)(2,1)S(1)}, bf16[512,512]{1,0:T(8,128)(2,1)}, u32[]{:S(2)}) %copy-start) | copy-done | bytes 524312
  2.5 0.0 copy-start.1
  2.5 0.9 %copy-done.1 = f32[128,512]{1,0:T(8,128)S(1)} copy-done((f32[128,512]{1,0:T(8,128)S(1)}, f32[128,512]{1,0:T(8,128)}, u32[]{:S(2)}) %copy-start.1) | copy-done | bytes 262168
  3.5 0.0 copy-start.2
  3.5 0.9 %copy-done.2 = bf16[2,256,256]{2,1,0:T(8,128)(2,1)S(1)} copy-done((bf16[2,256,256]{2,1,0:T(8,128)(2,1)S(1)}, bf16[2,256,256]{2,1,0:T(8,128)(2,1)}, u32[]{:S(2)}) %copy-start.2) | copy-done | bytes 262168
  4.4 0.0 copy-start.3
  4.4 0.9 %copy-done.3 = bf16[2,256,256]{2,1,0:T(8,128)(2,1)S(1)} copy-done((bf16[2,256,256]{2,1,0:T(8,128)(2,1)S(1)}, bf16[2,256,256]{2,1,0:T(8,128)(2,1)}, u32[]{:S(2)}) %copy-start.3) | copy-done | bytes 262168
  5.4 0.0 copy-start.4
  5.4 0.9 %copy-done.4 = bf16[1,128,512]{2,1,0:T(8,128)(2,1)S(1)} copy-done((bf16[1,128,512]{2,1,0:T(8,128)(2,1)S(1)}, bf16[1,128,512]{2,1,0:T(8,128)(2,1)}, u32[]{:S(2)}) %copy-start.4) | copy-done | bytes 131096
  6.3 0.0 copy-start.5
  6.3 0.9 %copy-done.5 = bf16[1,128,512]{2,1,0:T(8,128)(2,1)S(1)} copy-done((bf16[1,128,512]{2,1,0:T(8,128)(2,1)S(1)}, bf16[1,128,512]{2,1,0:T(8,128)(2,1)}, u32[]{:S(2)}) %copy-start.5) | copy-done | bytes 131096
  7.2 0.0 copy-start.6
  7.2 0.9 %copy-done.6 = bf16[1,128,512]{2,1,0:T(8,128)(2,1)S(1)} copy-done((bf16[1,128,512]{2,1,0:T(8,128)(2,1)S(1)}, bf16[1,128,512]{2,1,0:T(8,128)(2,1)}, u32[]{:S(2)}) %copy-start.6) | copy-done | bytes 131096
  8.1 0.0 copy-start.7
  8.1 0.9 %copy-done.7 = bf16[1,128,512]{2,1,0:T(8,128)(2,1)S(1)} copy-done((bf16[1,128,512]{2,1,0:T(8,128)(2,1)S(1)}, bf16[1,128,512]{2,1,0:T(8,128)(2,1)}, u32[]{:S(2)}) %copy-start.7) | copy-done | bytes 131096
  9.0 0.0 copy-start.9
  9.0 0.8 %copy-done.9 = f32[2,64,128]{2,1,0:T(8,128)S(1)} copy-done((f32[2,64,128]{2,1,0:T(8,128)S(1)}, f32[2,64,128]{2,1,0:T(8,128)}, u32[]{:S(2)}) %copy-start.9) | copy-done | bytes 65560
  9.8 0.0 copy-start.10
  9.8 0.8 %copy-done.10 = bf16[128,192]{1,0:T(8,128)(2,1)S(1)} copy-done((bf16[128,192]{1,0:T(8,128)(2,1)S(1)}, bf16[128,192]{1,0:T(8,128)(2,1)}, u32[]{:S(2)}) %copy-start.10) | copy-done | bytes 49176
  10.7 0.0 copy-start.11
  10.7 0.8 %copy-done.11 = bf16[64,384]{1,0:T(8,128)(2,1)S(1)} copy-done((bf16[64,384]{1,0:T(8,128)(2,1)S(1)}, bf16[64,384]{1,0:T(8,128)(2,1)}, u32[]{:S(2)}) %copy-start.11) | copy-done | bytes 49176
  11.5 54.6 %shard_map.164 = (bf16[128,512]{1,0:T(8,128)(2,1)S(1)}, bf16[128,512]{1,0:T(8,128)(2,1)S(1)}, bf16[128,512]{1,0:T(8,128)(2,1)S(1)}, f32[16,512]{1,0:T(8,128)S(1)}, f32[128,512]{1,0:T(8,128)S(1)}) custom-call(bf16[128,512]{1,0:T(8,128)(2,1)S(1)} %bitcast.8, bf16[128,512]{1,0:T(8,128)(2,1)S(1)} %bitcast.9, bf16[128,512]{1,0:T(8,128)(2,1)S(1)} %bitcast.10, ...), custom_call_target="tpu_custom_call" | custom-call | tf_op jit(solution)/shard_map/pallas_call | solution.py:389
  66.1 0.6 reshape.17
  66.7 0.7 copy.22
  67.4 0.7 copy.23
  68.0 0.7 copy.24
  68.7 0.7 %copy.25 = f32[128,512]{1,0:T(8,128)} copy(f32[128,512]{1,0:T(8,128)S(1)} %get-tuple-element.24) | data formatting | bytes 524288
Async XLA Ops:
  0.6 0.8 %copy-start.8 = (bf16[256,128]{1,0:T(8,128)(2,1)S(1)}, bf16[256,128]{1,0:T(8,128)(2,1)}, u32[]{:S(2)}) copy-start(bf16[256,128]{1,0:T(8,128)(2,1)} %constant.20.clone.pick1_ref) | copy-start | bytes 196612
  1.5 1.0 %copy-start = (bf16[512,512]{1,0:T(8,128)(2,1)S(1)}, bf16[512,512]{1,0:T(8,128)(2,1)}, u32[]{:S(2)}) copy-start(bf16[512,512]{1,0:T(8,128)(2,1)} %constant.19.clone.pick_ref) | copy-start | bytes 1572868
  2.5 0.9 %copy-start.1 = (f32[128,512]{1,0:T(8,128)S(1)}, f32[128,512]{1,0:T(8,128)}, u32[]{:S(2)}) copy-start(f32[128,512]{1,0:T(8,128)} %filt_ref.1) | copy-start | bytes 786436
  3.5 0.9 %copy-start.2 = (bf16[2,256,256]{2,1,0:T(8,128)(2,1)S(1)}, bf16[2,256,256]{2,1,0:T(8,128)(2,1)}, u32[]{:S(2)}) copy-start(bf16[2,256,256]{2,1,0:T(8,128)(2,1)} %constant.17.clone.inv_ref) | copy-start | bytes 786436
  4.4 0.9 %copy-start.3 = (bf16[2,256,256]{2,1,0:T(8,128)(2,1)S(1)}, bf16[2,256,256]{2,1,0:T(8,128)(2,1)}, u32[]{:S(2)}) copy-start(bf16[2,256,256]{2,1,0:T(8,128)(2,1)} %constant.16.clone.fwd_ref) | copy-start | bytes 786436
  5.4 0.9 %copy-start.4 = (bf16[1,128,512]{2,1,0:T(8,128)(2,1)S(1)}, bf16[1,128,512]{2,1,0:T(8,128)(2,1)}, u32[]{:S(2)}) copy-start(bf16[1,128,512]{2,1,0:T(8,128)(2,1)} %param.13) | copy-start | bytes 393220
  6.3 0.9 %copy-start.5 = (bf16[1,128,512]{2,1,0:T(8,128)(2,1)S(1)}, bf16[1,128,512]{2,1,0:T(8,128)(2,1)}, u32[]{:S(2)}) copy-start(bf16[1,128,512]{2,1,0:T(8,128)(2,1)} %param.14) | copy-start | bytes 393220
  7.2 0.9 %copy-start.6 = (bf16[1,128,512]{2,1,0:T(8,128)(2,1)S(1)}, bf16[1,128,512]{2,1,0:T(8,128)(2,1)}, u32[]{:S(2)}) copy-start(bf16[1,128,512]{2,1,0:T(8,128)(2,1)} %param.15) | copy-start | bytes 393220
  8.1 0.9 %copy-start.7 = (bf16[1,128,512]{2,1,0:T(8,128)(2,1)S(1)}, bf16[1,128,512]{2,1,0:T(8,128)(2,1)}, u32[]{:S(2)}) copy-start(bf16[1,128,512]{2,1,0:T(8,128)(2,1)} %param.18) | copy-start | bytes 393220
  9.0 0.8 %copy-start.9 = (f32[2,64,128]{2,1,0:T(8,128)S(1)}, f32[2,64,128]{2,1,0:T(8,128)}, u32[]{:S(2)}) copy-start(f32[2,64,128]{2,1,0:T(8,128)} %constant.18.clone.tw_ref) | copy-start | bytes 196612
  9.8 0.8 %copy-start.10 = (bf16[128,192]{1,0:T(8,128)(2,1)S(1)}, bf16[128,192]{1,0:T(8,128)(2,1)}, u32[]{:S(2)}) copy-start(bf16[128,192]{1,0:T(8,128)(2,1)} %constant.14.clone.first_ref) | copy-start | bytes 147460
  10.7 0.8 %copy-start.11 = (bf16[64,384]{1,0:T(8,128)(2,1)S(1)}, bf16[64,384]{1,0:T(8,128)(2,1)}, u32[]{:S(2)}) copy-start(bf16[64,384]{1,0:T(8,128)(2,1)} %constant.15.clone.last_ref) | copy-start | bytes 147460
where the time goes:
time: 69.9 us; the launch traced here: 69.4 us
  Pallas kernels  54.6 us (78%)
  local copies, waits for them, and re-layouts  14.1 us (20%)
    pallas_call x1, Pallas kernels, per_device(): pl.pallas_call(kernel, out_shape=(shape((rows, channels), BF16), shape((r...  54.6 us
    unnamed x28, local copies, waits for them, and re-layouts  12.7 us

commit v1 on v0

v1 whole, which is shorter than its diff:
```python
import functools
import math

import jax
import jax.numpy as jnp
import numpy as np
from jax import lax
from jax.experimental import pallas as pl
from jax.experimental.pallas import tpu as pltpu
from jax.sharding import PartitionSpec as P

MESH = pl.DeviceIdType.MESH
F32 = jnp.float32
BF16 = jnp.bfloat16

NZ, NPLANE, NCTX = 8, 16, 64
GROUP = NZ * NPLANE
CHAN = 4
SEQ = 2
POS = 128
ROWS = 16


def split_np(table):
    high = table.astype(jnp.bfloat16)
    low = (table - high.astype(np.float64)).astype(jnp.bfloat16)
    return high, low


@functools.cache
def tables():
    length = NCTX * POS
    a = np.arange(NCTX, dtype=np.float64)
    b = np.arange(POS, dtype=np.float64)
    outer = 2 * np.pi * np.outer(a, a + 0.25) / NCTX
    turn = 2 * np.pi * np.outer(a + 0.25, b) / length
    inner = 2 * np.pi * (np.outer(b, b) % POS) / POS
    first = np.concatenate([np.cos(outer.T), -np.sin(outer.T)], axis=0)
    high, low = split_np(first)
    first_cat = np.concatenate([high, low, high], axis=1)
    scale = 1.0 / (length * math.sqrt(length))
    last = np.concatenate([np.cos(outer), -np.sin(outer)], axis=1) * scale
    high, low = split_np(last)
    last_cat = np.concatenate([high, low, high], axis=1)
    c, s = np.cos(inner), np.sin(inner)
    forward = np.stack(split_np(np.block([[c, -s], [s, c]])))
    inverse = np.stack(split_np(np.block([[c, s], [-s, c]])))
    twiddle = np.stack([np.cos(turn), np.sin(turn)]).astype(np.float32)
    pick = np.zeros((32, 4, CHAN, 4, POS), np.float32)
    for g in range(32):
        for f in range(4):
            for i in range(CHAN):
                pick[g, f, i, f, CHAN * g + i] = 1
    pick = pick.reshape(512, 512).astype(jnp.bfloat16)
    return first_cat, last_cat, forward, inverse, twiddle, pick


def split(x):
    high = x.astype(BF16)
    return high, (x - high.astype(F32)).astype(BF16)


def dot(a, b):
    return jnp.dot(a, b, preferred_element_type=F32)


def dot_nt(a, b):
    return lax.dot_general(a, b, (((1,), (1,)), ((), ())), preferred_element_type=F32)


def stack_split(x):
    high, low = split(x)
    return jnp.concatenate([high, high, low], axis=0)


def wide_dot(x, table):
    high, low = split(x)
    return dot(high, table[0]) + (dot(high, table[1]) + dot(low, table[0]))


def wrap(v, n):
    return jnp.where(v >= n, v - n, v)


def kernel(
    q_hbm, k_hbm, v_hbm, c_hbm, filt_hbm, taps_hbm, first_hbm, last_hbm, fwd_hbm, inv_hbm, tw_hbm, pick_hbm,
    rrecv, tap_recv,
    q_ref, k_ref, v_ref, c_ref, filt_ref, taps_ref, first_ref, last_ref, fwd_ref, inv_ref, tw_ref, pick_ref,
    send_buf, recv_buf, fsend, frecv, raw, fraw, spec, hspec, keep, pack, rsend,
    sib_send, sib_recv, tap_rows, tap_own, tap_sib, tap_send,
    load_sems, send_sem, recv_sem, fsend_sem, frecv_sem, rsend_sem, rrecv_sem,
    sib_sems, tap_sems, plane_sem,
):
    dp, cx = lax.axis_index("dp"), lax.axis_index("ctx")
    zh, core = dp // 2, lax.rem(dp, 2)
    y, zl, x = cx // 16, lax.rem(cx // 4, 4), lax.rem(cx, 4)
    z = zh * 4 + zl
    me = zh * NCTX + cx
    xs = [wrap(x + dx, 4) for dx in range(4)]

    def place(zt, yt, xt, core_t):
        half = zt // 4
        ctx = yt * 16 + (zt - 4 * half) * 4 + xt
        return (half * 2 + core_t, ctx), half * NCTX + ctx

    def over(planes, act):
        bases = []
        for zt, own in planes:
            half = zt // 4
            bases.append((half * 2 + core, (zt - 4 * half) * 4, half * NCTX, own))

        def row(dy, carry, skip=False):
            yt = wrap(y + dy, 4) * 16
            for dx in range(4):
                for n, (dp_t, zrow, owner, own) in enumerate(bases):
                    if own and skip and dx == 0:
                        continue
                    ctx = yt + zrow + xs[dx]
                    act(n, (dp_t, ctx), owner + ctx)
            return carry

        if any(own for _, own in planes):
            row(0, 0, True)
            lax.fori_loop(1, 4, row, 0)
        else:
            lax.fori_loop(0, 4, row, 0)

    def plane_of(k):
        return wrap(z + k, NZ)

    sibling = (zh * 2 + (1 - core), cx)

    barrier = pltpu.get_barrier_semaphore()

    def signal_to(device, sem):
        pl.semaphore_signal(sem, inc=1, device_id=device, device_id_type=MESH)

    columns = [place(plane_of(k), y, x, core)[0] for k in range(NZ)]
    for k in (4, 3, 5, 2, 6, 1, 7):
        signal_to(columns[k], barrier)
    over([(z, True)], lambda n, to, owner: signal_to(to, barrier))
    signal_to(sibling, barrier)

    loads = [
        pltpu.make_async_copy(source, target, load_sems.at[n])
        for n, (source, target) in enumerate([
            (pick_hbm, pick_ref), (q_hbm, q_ref), (k_hbm, k_ref), (v_hbm, v_ref), (c_hbm, c_ref),
            (filt_hbm, filt_ref), (first_hbm, first_ref), (fwd_hbm, fwd_ref), (tw_hbm, tw_ref),
            (taps_hbm, taps_ref), (inv_hbm, inv_ref), (last_hbm, last_ref),
        ])
    ]
    for load in loads:
        load.start()
    for load in loads[:5]:
        load.wait()

    for j in range(4):
        lanes = slice(j * POS, (j + 1) * POS)
        fields = jnp.concatenate([q_ref[:, lanes], k_ref[:, lanes], v_ref[:, lanes], c_ref[:, lanes]], axis=1)
        rows = dot_nt(pick_ref[...], fields).astype(BF16)
        send_buf[pl.ds(j * 32, 32)] = rows.reshape(32, ROWS, POS)
    loads[5].wait()
    for j in range(4):
        lanes = slice(j * POS, (j + 1) * POS)
        high, low = split(filt_ref[:, lanes])
        pick_one = pick_ref[:, :POS]
        rows = dot_nt(pick_one, high) + dot_nt(pick_one, low)
        fsend[pl.ds(j * 32, 32)] = rows.reshape(32, ROWS, POS)[:, :CHAN, :]

    own = pltpu.make_async_copy(send_buf.at[me], recv_buf.at[me], recv_sem.at[zh])
    own.start()
    fown = pltpu.make_async_copy(fsend.at[me], frecv.at[cx], frecv_sem)
    fown.start()

    pl.semaphore_wait(barrier, NPLANE - 1 + NZ - 1 + 1)
    for k in (4, 3, 5, 2, 6, 1, 7):
        signal_to(columns[k], plane_sem.at[NZ - k])

    near = (0, 1, 2, 7)
    for planes in ((0,), (7, 1), (6, 2), (5, 3), (4,)):
        for k in planes:
            if k:
                pl.semaphore_wait(plane_sem.at[k], 1)

        def send(n, to, owner, planes=planes):
            if planes[n] in near:
                pltpu.make_async_remote_copy(
                    src_ref=fsend.at[owner], dst_ref=frecv.at[cx], send_sem=fsend_sem, recv_sem=frecv_sem,
                    device_id=to, device_id_type=MESH,
                ).start()
            pltpu.make_async_remote_copy(
                src_ref=send_buf.at[owner], dst_ref=recv_buf.at[me], send_sem=send_sem, recv_sem=recv_sem.at[zh],
                device_id=to, device_id_type=MESH,
            ).start()

        over([(plane_of(k), k == 0) for k in planes], send)

    def wait_bytes(ref, sem):
        pltpu.make_async_copy(ref, ref, sem).wait()

    row_id = lax.broadcasted_iota(jnp.int32, (NCTX, POS), 0)
    lane_id = lax.broadcasted_iota(jnp.int32, (NCTX, POS), 1)

    def before(v, s):
        turned = pltpu.roll(v, s, 1)
        carried = jnp.where(row_id == 0, 0.0, pltpu.roll(turned, 1, 0))
        return jnp.where(lane_id < s, carried, turned)

    def after(v, s):
        turned = pltpu.roll(v, POS - s, 1)
        carried = jnp.where(row_id == NCTX - 1, 0.0, pltpu.roll(turned, NCTX - 1, 0))
        return jnp.where(lane_id >= POS - s, carried, turned)

    for load in loads[6:]:
        load.wait()
    channel = lax.broadcasted_iota(jnp.int32, (3, GROUP * CHAN), 1)
    tap_values = [
        [jnp.sum(jnp.where(channel == me * CHAN + i, taps_ref[branch], 0.0), axis=1, keepdims=True) for i in range(CHAN)]
        for branch in range(3)
    ]

    def tap(branch, j, i):
        return tap_values[branch][i][j:j + 1]

    def field(h, f, i):
        return raw[h, pl.ds(f * CHAN + i, NCTX, ROWS), :]

    cos, sin = tw_ref[0], tw_ref[1]

    def spectrum(values):
        turned = dot(first_ref[...], stack_split(jnp.concatenate(values, axis=1)))
        parts = []
        for n in range(len(values)):
            re, im = turned[:NCTX, n * POS:(n + 1) * POS], turned[NCTX:, n * POS:(n + 1) * POS]
            parts.append(jnp.concatenate([re * cos + im * sin, im * cos - re * sin], axis=1))
        return wide_dot(jnp.concatenate(parts, axis=0), fwd_ref)

    def signal(spectra):
        joined = jnp.concatenate([jnp.concatenate(s, axis=1) for s in spectra], axis=0)
        turned = wide_dot(joined, inv_ref)
        parts = []
        for n in range(len(spectra)):
            re, im = turned[n * NCTX:(n + 1) * NCTX, :POS], turned[n * NCTX:(n + 1) * NCTX, POS:]
            parts.append(jnp.concatenate([re * cos - im * sin, re * sin + im * cos], axis=0))
        return dot(last_ref[...], stack_split(jnp.concatenate(parts, axis=1)))

    def halves(ref, n):
        return ref[n * NCTX:(n + 1) * NCTX, :POS], ref[n * NCTX:(n + 1) * NCTX, POS:]

    for h in (zh, 1 - zh):
        wait_bytes(recv_buf.at[pl.ds(h * NCTX, NCTX)], recv_sem.at[h])
        raw[h] = recv_buf[pl.ds(h * NCTX, NCTX)].astype(F32).reshape(NCTX * ROWS, POS)
        values = []
        for i in range(CHAN):
            feats = []
            for branch in range(3):
                v = field(h, branch, i)
                feats.append(
                    tap(branch, 0, i) * v + tap(branch, 1, i) * before(v, 1) + tap(branch, 2, i) * before(v, 2)
                )
            keep[h, i, 0] = feats[1]
            keep[h, i, 1] = feats[2]
            values += [feats[1] * feats[2], feats[0] * field(h, 3, i)]
        spec[h] = spectrum(values)

    corrs = []
    for i in range(CHAN):
        re = im = 0.0
        for h in range(SEQ):
            mr, mi = halves(spec.at[h], 2 * i)
            gr, gi = halves(spec.at[h], 2 * i + 1)
            re, im = re + (mr * gr + mi * gi), im + (mr * gi - mi * gr)
        corrs.append((re, im))
    sib_send[...] = signal(corrs)
    sib = pltpu.make_async_remote_copy(
        src_ref=sib_send, dst_ref=sib_recv, send_sem=sib_sems.at[0], recv_sem=sib_sems.at[1],
        device_id=sibling, device_id_type=MESH,
    )
    sib.start()

    wait_bytes(frecv, frecv_sem)
    filt = frecv[...]
    fraw[...] = jnp.concatenate([filt, jnp.zeros_like(filt)], axis=1).reshape(NCTX * 8, POS)
    hspec[...] = spectrum([fraw[pl.ds(i, NCTX, 8), :] for i in range(CHAN)])

    tap_rows[...] = jnp.zeros_like(tap_rows)
    for step, h in enumerate((1 - zh, zh)):
        spectra = []
        for i in range(CHAN):
            fr, fi = halves(hspec, i)
            mr, mi = halves(spec.at[h], 2 * i)
            gr, gi = halves(spec.at[h], 2 * i + 1)
            spectra += [(fr * mr - fi * mi, fr * mi + fi * mr), (fr * gr + fi * gi, fr * gi - fi * gr)]
        back = signal(spectra)
        grads = []
        for i in range(CHAN):
            conv = back[:, 2 * i * POS:(2 * i + 1) * POS]
            adj = back[:, (2 * i + 1) * POS:(2 * i + 2) * POS]
            grads.append([field(h, 3, i) * conv, adj * keep[h, i, 1], adj * keep[h, i, 0]])
            for branch in range(3):
                d = grads[i][branch]
                pack[pl.ds(branch * CHAN + i, NCTX, ROWS), :] = (
                    tap(branch, 0, i) * d + tap(branch, 1, i) * after(d, 1) + tap(branch, 2, i) * after(d, 2)
                )
        if step == 0:
            sib.wait_recv()
            for i in range(CHAN):
                pack[pl.ds(3 * CHAN + i, NCTX, ROWS), :] = (
                    sib_send[:, i * POS:(i + 1) * POS] + sib_recv[:, i * POS:(i + 1) * POS]
                )
        rsend[pl.ds(h * NCTX, NCTX)] = pack[...].reshape(NCTX, ROWS, POS).astype(BF16)

        def give(n, to, owner):
            pltpu.make_async_remote_copy(
                src_ref=rsend.at[owner], dst_ref=rrecv.at[me], send_sem=rsend_sem, recv_sem=rrecv_sem,
                device_id=to, device_id_type=MESH,
            ).start()

        over([(h * 4 + wrap(zl + t, 4), step == 1 and t == 0) for t in range(4)], give)
        for i in range(CHAN):
            for branch in range(3):
                d, v = grads[i][branch], field(h, branch, i)
                for j in range(3):
                    term = d * (before(v, j) if j else v)
                    row = (branch * 3 + j) * CHAN + i
                    tap_rows[row:row + 1, :] += jnp.sum(term, axis=0, keepdims=True)
    rown = pltpu.make_async_copy(rsend.at[me], rrecv.at[me], rrecv_sem)
    rown.start()

    ones = jnp.ones((8, POS), F32)
    scale = 1.0 / math.sqrt(SEQ * 2 * NCTX * POS)
    sums = lax.dot_general(
        ones, tap_rows[...], (((1,), (1,)), ((), ())), precision=lax.Precision.HIGHEST, preferred_element_type=F32
    )
    tap_own[...] = sums[0:1] * scale
    tap_sibling = pltpu.make_async_remote_copy(
        src_ref=tap_own, dst_ref=tap_sib, send_sem=tap_sems.at[0], recv_sem=tap_sems.at[1],
        device_id=sibling, device_id_type=MESH,
    )
    tap_sibling.start()
    tap_sibling.wait_recv()
    tap_send[...] = tap_own[...] + tap_sib[...]
    town = pltpu.make_async_copy(tap_send, tap_recv.at[me], tap_sems.at[3])
    town.start()

    def tell(n, to, owner):
        pltpu.make_async_remote_copy(
            src_ref=tap_send, dst_ref=tap_recv.at[me], send_sem=tap_sems.at[2], recv_sem=tap_sems.at[3],
            device_id=to, device_id_type=MESH,
        ).start()

    over([((1 - zh) * 4 + wrap(zl + t, 4), False) for t in range(4)], tell)
    over([(zh * 4 + wrap(zl + t, 4), t == 0) for t in range(4)], tell)

    wait_bytes(send_buf.at[pl.ds(0, GROUP - 1)], send_sem)
    wait_bytes(fsend.at[pl.ds(0, NCTX - 1)], fsend_sem)
    sib.wait_send()
    tap_sibling.wait_send()

    wait_bytes(rrecv, rrecv_sem)
    wait_bytes(tap_recv, tap_sems.at[3])
    wait_bytes(rsend.at[pl.ds(0, GROUP - 1)], rsend_sem)
    wait_bytes(tap_recv.at[pl.ds(0, GROUP - 1)], tap_sems.at[2])


def finish(
    rows_hbm, taps_hbm, pick_hbm, gq_hbm, gk_hbm, gv_hbm, gt_hbm, gf_hbm,
    rows_ref, taps_ref, pick_ref, gq_ref, gk_ref, gv_ref, gt_ref, gf_ref, load_sems, out_sems,
):
    load_pick = pltpu.make_async_copy(pick_hbm, pick_ref, load_sems.at[0])
    load_pick.start()
    loads = [
        pltpu.make_async_copy(rows_hbm.at[pl.ds(j * 32, 32)], rows_ref.at[pl.ds(j * 32, 32)], load_sems.at[1 + j])
        for j in range(4)
    ]
    for load in loads:
        load.start()
    load_taps = pltpu.make_async_copy(taps_hbm, taps_ref, load_sems.at[5])
    load_taps.start()
    load_pick.wait()
    outs = []
    for j in range(4):
        lanes = pl.ds(j * POS, POS)
        loads[j].wait()
        rows = rows_ref[pl.ds(j * 32, 32)].reshape(512, POS)
        out = lax.dot_general(rows, pick_ref[...], (((0,), (0,)), ((), ())), preferred_element_type=F32)
        gq_ref[:, lanes] = out[:, :POS].astype(BF16)
        gk_ref[:, lanes] = out[:, POS:2 * POS].astype(BF16)
        gv_ref[:, lanes] = out[:, 2 * POS:3 * POS].astype(BF16)
        gf_ref[:, lanes] = out[:, 3 * POS:]
        for n, (source, target) in enumerate([(gq_ref, gq_hbm), (gk_ref, gk_hbm), (gv_ref, gv_hbm), (gf_ref, gf_hbm)]):
            outs.append(pltpu.make_async_copy(source.at[:, lanes], target.at[:, lanes], out_sems.at[4 * j + n]))
            outs[-1].start()

    load_taps.wait()
    taps_all = taps_ref[...].reshape(GROUP, POS)
    total = jnp.zeros((16, GROUP * CHAN), F32)
    for i in range(CHAN):
        pick_row = (
            lax.broadcasted_iota(jnp.int32, (16, POS), 1)
            == CHAN * lax.broadcasted_iota(jnp.int32, (16, POS), 0) + i
        ).astype(F32)
        spread = (
            lax.broadcasted_iota(jnp.int32, (GROUP, GROUP * CHAN), 1)
            == CHAN * lax.broadcasted_iota(jnp.int32, (GROUP, GROUP * CHAN), 0) + i
        ).astype(F32)
        rows = lax.dot_general(
            pick_row, taps_all, (((1,), (1,)), ((), ())),
            precision=lax.Precision.HIGHEST, preferred_element_type=F32,
        )
        total += jnp.dot(rows, spread, precision=lax.Precision.HIGHEST, preferred_element_type=F32)
    for branch in range(3):
        gt_ref[branch] = total[branch * 3:branch * 3 + 3]
    outs.append(pltpu.make_async_copy(gt_ref, gt_hbm, out_sems.at[16]))
    outs[-1].start()
    for out in outs:
        out.wait()


def per_device(query_in, key_in, value_in, short_taps, long_filter, cotangent):
    rows, channels = query_in.shape[1:]
    hbm = pl.BlockSpec(memory_space=pltpu.HBM)
    shape = jax.ShapeDtypeStruct
    results = (
        shape((rows, channels), BF16),
        shape((rows, channels), BF16),
        shape((rows, channels), BF16),
        shape(short_taps.shape, F32),
        shape((rows, channels), F32),
    )
    constants = [jnp.asarray(t) for t in tables()]
    operands = [query_in[0], key_in[0], value_in[0], cotangent[0], long_filter, short_taps, *constants]
    scratch = [pltpu.VMEM(v.shape, v.dtype) for v in operands] + [
        pltpu.VMEM((GROUP, ROWS, POS), BF16),
        pltpu.VMEM((GROUP, ROWS, POS), BF16),
        pltpu.VMEM((GROUP, CHAN, POS), F32),
        pltpu.VMEM((NCTX, CHAN, POS), F32),
        pltpu.VMEM((SEQ, NCTX * ROWS, POS), F32),
        pltpu.VMEM((NCTX * 8, POS), F32),
        pltpu.VMEM((SEQ, 2 * CHAN * NCTX, 2 * POS), F32),
        pltpu.VMEM((CHAN * NCTX, 2 * POS), F32),
        pltpu.VMEM((SEQ, CHAN, 2, NCTX, POS), F32),
        pltpu.VMEM((NCTX * ROWS, POS), F32),
        pltpu.VMEM((GROUP, ROWS, POS), BF16),
        pltpu.VMEM((NCTX, CHAN * POS), F32),
        pltpu.VMEM((NCTX, CHAN * POS), F32),
        pltpu.VMEM((POS, POS), F32),
        pltpu.VMEM((1, POS), F32),
        pltpu.VMEM((1, POS), F32),
        pltpu.VMEM((1, POS), F32),
        pltpu.SemaphoreType.DMA((len(operands),)),
        pltpu.SemaphoreType.DMA,
        pltpu.SemaphoreType.DMA((SEQ,)),
        pltpu.SemaphoreType.DMA,
        pltpu.SemaphoreType.DMA,
        pltpu.SemaphoreType.DMA,
        pltpu.SemaphoreType.DMA,
        pltpu.SemaphoreType.DMA((2,)),
        pltpu.SemaphoreType.DMA((4,)),
        pltpu.SemaphoreType.REGULAR((NZ,)),
    ]
    params = functools.partial(pltpu.CompilerParams, vmem_limit_bytes=63 * 1024 * 1024)
    held = pl.pallas_call(
        kernel,
        out_shape=(shape((GROUP, ROWS, POS), BF16), shape((GROUP, 1, POS), F32)),
        in_specs=[hbm] * len(operands),
        out_specs=[hbm] * 2,
        scratch_shapes=scratch,
        compiler_params=params(collective_id=0, has_side_effects=True),
    )(*operands)
    inner = [*held, operands[-1]]
    grad_query, grad_key, grad_value, grad_taps, grad_filter = pl.pallas_call(
        finish,
        out_shape=results,
        in_specs=[hbm] * 3,
        out_specs=[hbm] * 5,
        scratch_shapes=[pltpu.VMEM(v.shape, v.dtype) for v in (*inner, *results)]
        + [pltpu.SemaphoreType.DMA((6,)), pltpu.SemaphoreType.DMA((17,))],
        compiler_params=params(),
    )(*inner)
    return (grad_query[None], grad_key[None], grad_value[None], grad_taps, grad_filter)


def solution(mesh):
    seq = P("dp", "ctx", None)
    return jax.shard_map(
        per_device,
        mesh=mesh,
        in_specs=(seq, seq, seq, P(), P("ctx", None), seq),
        out_specs=(seq, seq, seq, P(), P("ctx", None)),
        check_vma=False,
    )
```

time: 69.9 us -> 55.7 us (0.80)
  local copies, waits for them, and re-layouts: 14.1 us -> 0 us
    unnamed x28 -> x0, local copies, waits for them, and re-layouts: 12.7 us -> none
    reshape x2 -> x0, local copies, waits for them, and re-layouts: 1.4 us -> none  [the longest x1 0.78 us: per_device(): short_taps.reshape(9, channels)]
    pallas_call x1 -> x2, Pallas kernels: 54.6 us -> 54.9 us  [the longest x1 50.5 us: per_device(): pl.pallas_call(kernel, out_shape=(shape((GROUP, ROWS, POS), BF16), shape(...]
where the time goes in v1:
time: 55.7 us; the launch traced here: 55.6 us
  Pallas kernels  54.9 us (99%)
  between operations  0.64 us (1%)
    pallas_call x1, Pallas kernels, per_device(): pl.pallas_call(kernel, out_shape=(shape((GROUP, ROWS, POS), BF16), shape(...  50.5 us
    pallas_call x1, Pallas kernels, per_device(): pl.pallas_call(finish, out_shape=results, in_specs=[hbm] * 3, out_specs=[...  4.4 us

profile of v1, /device:TPU:1, one launch (start us, length us, event | category | flops | bytes accessed | tf_op | source)
XLA Modules:
  0.0 55.6 jit_solution(946099942966989152)
XLA Ops:
  0.6 50.5 %shard_map.155 = (bf16[128,16,128]{2,1,0:T(8,128)(2,1)}, f32[128,1,128]{2,1,0:T(1,128)}) custom-call(bf16[128,512]{1,0:T(8,128)(2,1)} %bitcast.7, bf16[128,512]{1,0:T(8,128)(2,1)} %bitcast.8, bf16[128,512]{1,0:T(8,128)(2,1)} %bitcast.9, bf16[128,512]{1,0:T(8,128)(2,1)} %bitcast.10, f32[128,512]{1,0:T(8,128)} %filt_hbm.1, f32[3,3,512]{2,1,0:T(4,128)} %taps_hbm.1, ...), custom_call_target="tpu_custom_call" | custom-call | tf_op jit(solution)/shard_map/pallas_call | solution.py:463
  51.2 4.4 %shard_map.156 = (bf16[128,512]{1,0:T(8,128)(2,1)}, bf16[128,512]{1,0:T(8,128)(2,1)}, bf16[128,512]{1,0:T(8,128)(2,1)}, f32[3,3,512]{2,1,0:T(4,128)}, f32[128,512]{1,0:T(8,128)}) custom-call(bf16[128,16,128]{2,1,0:T(8,128)(2,1)} %get-tuple-element.12.rows_hbm, f32[128,1,128]{2,1,0:T(1,128)} %get-tuple-element.13.taps_hbm, ...), custom_call_target="tpu_custom_call" | custom-call | tf_op jit(solution)/shard_map/pallas_call | solution.py:472

commit v2 on v1

--- a/solution.py
+++ b/solution.py
@@ -1,4 +1,5 @@
 import functools
+import itertools
 import math
 
 import jax
@@ -19,6 +20,16 @@
 SEQ = 2
 POS = 128
 ROWS = 16
+REACH = 8
+
+
+def shell(reach):
+    hops = lambda d, n: min(d, n - d)
+    by_z = [
+        [(dx, dy, dz) for dy in range(4) for dx in range(4) if hops(dx, 4) + hops(dy, 4) + hops(dz, NZ) == reach]
+        for dz in (4, 3, 5, 2, 6, 1, 7, 0)
+    ]
+    return [d for row in itertools.zip_longest(*by_z) for d in row if d]
 
 
 def split_np(table):
@@ -96,7 +107,6 @@
     y, zl, x = cx // 16, lax.rem(cx // 4, 4), lax.rem(cx, 4)
     z = zh * 4 + zl
     me = zh * NCTX + cx
-    xs = [wrap(x + dx, 4) for dx in range(4)]
 
     def place(zt, yt, xt, core_t):
         half = zt // 4
@@ -111,7 +121,7 @@
 
         def row(dy, carry, skip=False):
             yt = wrap(y + dy, 4) * 16
-            for dx in range(4):
+            for dx in (2, 1, 3, 0):
                 for n, (dp_t, zrow, owner, own) in enumerate(bases):
                     if own and skip and dx == 0:
                         continue
@@ -135,10 +145,26 @@
     def signal_to(device, sem):
         pl.semaphore_signal(sem, inc=1, device_id=device, device_id_type=MESH)
 
-    columns = [place(plane_of(k), y, x, core)[0] for k in range(NZ)]
-    for k in (4, 3, 5, 2, 6, 1, 7):
-        signal_to(columns[k], barrier)
-    over([(z, True)], lambda n, to, owner: signal_to(to, barrier))
+    xs = [wrap(x + dx, 4) for dx in range(4)]
+    ys = [wrap(y + dy, 4) * 16 for dy in range(4)]
+    zs = []
+    for dz in range(NZ):
+        zt = plane_of(dz)
+        half = zt // 4
+        zs.append((half * 2 + core, (zt - 4 * half) * 4, half * NCTX))
+
+    def target(dx, dy, dz):
+        dp_t, zrow, first = zs[dz]
+        ctx = ys[dy] + zrow + xs[dx]
+        return (dp_t, ctx), first + ctx
+
+    columns = [target(0, 0, dz)[0] for dz in range(NZ)]
+    for dz in (4, 3, 5, 2, 6, 1, 7):
+        signal_to(columns[dz], barrier)
+    for dy in (2, 1, 3, 0):
+        for dx in (2, 1, 3, 0):
+            if dx or dy:
+                signal_to(target(dx, dy, 0)[0], barrier)
     signal_to(sibling, barrier)
 
     loads = [
@@ -162,9 +188,7 @@
     loads[5].wait()
     for j in range(4):
         lanes = slice(j * POS, (j + 1) * POS)
-        high, low = split(filt_ref[:, lanes])
-        pick_one = pick_ref[:, :POS]
-        rows = dot_nt(pick_one, high) + dot_nt(pick_one, low)
+        rows = dot_nt(pick_ref[:, :POS], filt_ref[:, lanes].astype(BF16)).astype(BF16)
         fsend[pl.ds(j * 32, 32)] = rows.reshape(32, ROWS, POS)[:, :CHAN, :]
 
     own = pltpu.make_async_copy(send_buf.at[me], recv_buf.at[me], recv_sem.at[zh])
@@ -173,27 +197,24 @@
     fown.start()
 
     pl.semaphore_wait(barrier, NPLANE - 1 + NZ - 1 + 1)
-    for k in (4, 3, 5, 2, 6, 1, 7):
-        signal_to(columns[k], plane_sem.at[NZ - k])
-
+    for dz in (4, 3, 5, 2, 6, 1, 7):
+        signal_to(columns[dz], plane_sem.at[NZ - dz])
     near = (0, 1, 2, 7)
-    for planes in ((0,), (7, 1), (6, 2), (5, 3), (4,)):
-        for k in planes:
-            if k:
-                pl.semaphore_wait(plane_sem.at[k], 1)
-
-        def send(n, to, owner, planes=planes):
-            if planes[n] in near:
+    plane = [(dx, dy) for dy in (2, 1, 3, 0) for dx in (2, 1, 3, 0)]
+    for dz in range(1, NZ):
+        pl.semaphore_wait(plane_sem.at[dz], 1)
+    for dx, dy in plane:
+        for d in [(dx, dy, dz) for dz in (4, 3, 5, 2, 6, 1, 7, 0) if dx or dy or dz]:
+            to, owner = target(*d)
+            pltpu.make_async_remote_copy(
+                src_ref=send_buf.at[owner], dst_ref=recv_buf.at[me], send_sem=send_sem, recv_sem=recv_sem.at[zh],
+                device_id=to, device_id_type=MESH,
+            ).start()
+            if d[2] in near:
                 pltpu.make_async_remote_copy(
                     src_ref=fsend.at[owner], dst_ref=frecv.at[cx], send_sem=fsend_sem, recv_sem=frecv_sem,
                     device_id=to, device_id_type=MESH,
                 ).start()
-            pltpu.make_async_remote_copy(
-                src_ref=send_buf.at[owner], dst_ref=recv_buf.at[me], send_sem=send_sem, recv_sem=recv_sem.at[zh],
-                device_id=to, device_id_type=MESH,
-            ).start()
-
-        over([(plane_of(k), k == 0) for k in planes], send)
 
     def wait_bytes(ref, sem):
         pltpu.make_async_copy(ref, ref, sem).wait()
@@ -246,6 +267,11 @@
 
     def halves(ref, n):
         return ref[n * NCTX:(n + 1) * NCTX, :POS], ref[n * NCTX:(n + 1) * NCTX, POS:]
+
+    wait_bytes(frecv, frecv_sem)
+    filt = frecv[...].astype(F32)
+    fraw[...] = jnp.concatenate([filt, jnp.zeros_like(filt)], axis=1).reshape(NCTX * 8, POS)
+    hspec[...] = spectrum([fraw[pl.ds(i, NCTX, 8), :] for i in range(CHAN)])
 
     for h in (zh, 1 - zh):
         wait_bytes(recv_buf.at[pl.ds(h * NCTX, NCTX)], recv_sem.at[h])
@@ -277,11 +303,6 @@
         device_id=sibling, device_id_type=MESH,
     )
     sib.start()
-
-    wait_bytes(frecv, frecv_sem)
-    filt = frecv[...]
-    fraw[...] = jnp.concatenate([filt, jnp.zeros_like(filt)], axis=1).reshape(NCTX * 8, POS)
-    hspec[...] = spectrum([fraw[pl.ds(i, NCTX, 8), :] for i in range(CHAN)])
 
     tap_rows[...] = jnp.zeros_like(tap_rows)
     for step, h in enumerate((1 - zh, zh)):
@@ -308,7 +329,14 @@
                 pack[pl.ds(3 * CHAN + i, NCTX, ROWS), :] = (
                     sib_send[:, i * POS:(i + 1) * POS] + sib_recv[:, i * POS:(i + 1) * POS]
                 )
-        rsend[pl.ds(h * NCTX, NCTX)] = pack[...].reshape(NCTX, ROWS, POS).astype(BF16)
+        def tap_terms():
+            for i in range(CHAN):
+                for branch in range(3):
+                    d, v = grads[i][branch], field(h, branch, i)
+                    for j in range(3):
+                        term = d * (before(v, j) if j else v)
+                        row = (branch * 3 + j) * CHAN + i
+                        tap_rows[row:row + 1, :] += jnp.sum(term, axis=0, keepdims=True)
 
         def give(n, to, owner):
             pltpu.make_async_remote_copy(
@@ -316,41 +344,39 @@
                 device_id=to, device_id_type=MESH,
             ).start()
 
-        over([(h * 4 + wrap(zl + t, 4), step == 1 and t == 0) for t in range(4)], give)
-        for i in range(CHAN):
-            for branch in range(3):
-                d, v = grads[i][branch], field(h, branch, i)
-                for j in range(3):
-                    term = d * (before(v, j) if j else v)
-                    row = (branch * 3 + j) * CHAN + i
-                    tap_rows[row:row + 1, :] += jnp.sum(term, axis=0, keepdims=True)
+        def give_all():
+            rsend[pl.ds(h * NCTX, NCTX)] = pack[...].reshape(NCTX, ROWS, POS).astype(BF16)
+            over([(h * 4 + wrap(zl + t, 4), step == 1 and t == 0) for t in range(4)], give)
+
+        if step == 0:
+            give_all()
+            tap_terms()
+        else:
+            tap_terms()
+            ones = jnp.ones((8, POS), BF16)
+            scale = 1.0 / math.sqrt(SEQ * 2 * NCTX * POS)
+            high, low = split(tap_rows[...])
+            tap_own[...] = (dot_nt(ones, high) + dot_nt(ones, low))[0:1] * scale
+            tap_sibling = pltpu.make_async_remote_copy(
+                src_ref=tap_own, dst_ref=tap_sib, send_sem=tap_sems.at[0], recv_sem=tap_sems.at[1],
+                device_id=sibling, device_id_type=MESH,
+            )
+            tap_sibling.start()
+            give_all()
+    tap_sibling.wait_recv()
+    tap_send[...] = tap_own[...] + tap_sib[...]
+    for dy in (2, 1, 3, 0):
+        for dx in (2, 1, 3, 0):
+            for dz in (4, 3, 5, 2, 6, 1, 7, 0):
+                if dx or dy or dz:
+                    pltpu.make_async_remote_copy(
+                        src_ref=tap_send, dst_ref=tap_recv.at[me], send_sem=tap_sems.at[2], recv_sem=tap_sems.at[3],
+                        device_id=target(dx, dy, dz)[0], device_id_type=MESH,
+                    ).start()
+    town = pltpu.make_async_copy(tap_send, tap_recv.at[me], tap_sems.at[3])
+    town.start()
     rown = pltpu.make_async_copy(rsend.at[me], rrecv.at[me], rrecv_sem)
     rown.start()
-
-    ones = jnp.ones((8, POS), F32)
-    scale = 1.0 / math.sqrt(SEQ * 2 * NCTX * POS)
-    sums = lax.dot_general(
-        ones, tap_rows[...], (((1,), (1,)), ((), ())), precision=lax.Precision.HIGHEST, preferred_element_type=F32
-    )
-    tap_own[...] = sums[0:1] * scale
-    tap_sibling = pltpu.make_async_remote_copy(
-        src_ref=tap_own, dst_ref=tap_sib, send_sem=tap_sems.at[0], recv_sem=tap_sems.at[1],
-        device_id=sibling, device_id_type=MESH,
-    )
-    tap_sibling.start()
-    tap_sibling.wait_recv()
-    tap_send[...] = tap_own[...] + tap_sib[...]
-    town = pltpu.make_async_copy(tap_send, tap_recv.at[me], tap_sems.at[3])
-    town.start()
-
-    def tell(n, to, owner):
-        pltpu.make_async_remote_copy(
-            src_ref=tap_send, dst_ref=tap_recv.at[me], send_sem=tap_sems.at[2], recv_sem=tap_sems.at[3],
-            device_id=to, device_id_type=MESH,
-        ).start()
-
-    over([((1 - zh) * 4 + wrap(zl + t, 4), False) for t in range(4)], tell)
-    over([(zh * 4 + wrap(zl + t, 4), t == 0) for t in range(4)], tell)
 
     wait_bytes(send_buf.at[pl.ds(0, GROUP - 1)], send_sem)
     wait_bytes(fsend.at[pl.ds(0, NCTX - 1)], fsend_sem)
@@ -377,6 +403,12 @@
         load.start()
     load_taps = pltpu.make_async_copy(taps_hbm, taps_ref, load_sems.at[5])
     load_taps.start()
+    row = lax.broadcasted_iota(jnp.int32, (CHAN * 16, POS), 0)
+    lane = lax.broadcasted_iota(jnp.int32, (CHAN * 16, POS), 1)
+    pick_row = (lane == CHAN * (row % 16) + row // 16).astype(F32).astype(BF16)
+    row = lax.broadcasted_iota(jnp.int32, (CHAN * GROUP, GROUP * CHAN), 0)
+    lane = lax.broadcasted_iota(jnp.int32, (CHAN * GROUP, GROUP * CHAN), 1)
+    spread = (lane == CHAN * (row % GROUP) + row // GROUP).astype(F32).astype(BF16)
     load_pick.wait()
     outs = []
     for j in range(4):
@@ -393,22 +425,11 @@
             outs[-1].start()
 
     load_taps.wait()
-    taps_all = taps_ref[...].reshape(GROUP, POS)
-    total = jnp.zeros((16, GROUP * CHAN), F32)
-    for i in range(CHAN):
-        pick_row = (
-            lax.broadcasted_iota(jnp.int32, (16, POS), 1)
-            == CHAN * lax.broadcasted_iota(jnp.int32, (16, POS), 0) + i
-        ).astype(F32)
-        spread = (
-            lax.broadcasted_iota(jnp.int32, (GROUP, GROUP * CHAN), 1)
-            == CHAN * lax.broadcasted_iota(jnp.int32, (GROUP, GROUP * CHAN), 0) + i
-        ).astype(F32)
-        rows = lax.dot_general(
-            pick_row, taps_all, (((1,), (1,)), ((), ())),
-            precision=lax.Precision.HIGHEST, preferred_element_type=F32,
-        )
-        total += jnp.dot(rows, spread, precision=lax.Precision.HIGHEST, preferred_element_type=F32)
+    high, low = split(taps_ref[...].reshape(GROUP, POS))
+    rows = dot_nt(pick_row, high) + dot_nt(pick_row, low)
+    high, low = split(jnp.concatenate([rows[i * 16:(i + 1) * 16] for i in range(CHAN)], axis=1))
+    both = dot(jnp.concatenate([high, low], axis=0), spread)
+    total = both[:16] + both[16:]
     for branch in range(3):
         gt_ref[branch] = total[branch * 3:branch * 3 + 3]
     outs.append(pltpu.make_async_copy(gt_ref, gt_hbm, out_sems.at[16]))
@@ -433,8 +454,8 @@
     scratch = [pltpu.VMEM(v.shape, v.dtype) for v in operands] + [
         pltpu.VMEM((GROUP, ROWS, POS), BF16),
         pltpu.VMEM((GROUP, ROWS, POS), BF16),
-        pltpu.VMEM((GROUP, CHAN, POS), F32),
-        pltpu.VMEM((NCTX, CHAN, POS), F32),
+        pltpu.VMEM((GROUP, CHAN, POS), BF16),
+        pltpu.VMEM((NCTX, CHAN, POS), BF16),
         pltpu.VMEM((SEQ, NCTX * ROWS, POS), F32),
         pltpu.VMEM((NCTX * 8, POS), F32),
         pltpu.VMEM((SEQ, 2 * CHAN * NCTX, 2 * POS), F32),

time: 55.7 us -> 54 us (0.969)
  Pallas kernels: 54.9 us -> 53.2 us
    pallas_call x1, Pallas kernels: 4.4 us -> 3.41 us  [per_device(): pl.pallas_call(finish, out_shape=results, in_specs=[hbm] * 3, out_specs=[...]
    pallas_call x1, Pallas kernels: 50.5 us -> 49.8 us  [per_device(): pl.pallas_call(kernel, out_shape=(shape((GROUP, ROWS, POS), BF16), shape(...]
where the time goes in v2:
time: 54 us; the launch traced here: 53.8 us
  Pallas kernels  53.2 us (99%)
  between operations  0.64 us (1%)
    pallas_call x1, Pallas kernels, per_device(): pl.pallas_call(kernel, out_shape=(shape((GROUP, ROWS, POS), BF16), shape(...  49.8 us
    pallas_call x1, Pallas kernels, per_device(): pl.pallas_call(finish, out_shape=results, in_specs=[hbm] * 3, out_specs=[...  3.41 us

profile of v2, /device:TPU:1, one launch (start us, length us, event | category | flops | bytes accessed | tf_op | source)
XLA Modules:
  0.0 53.8 jit_solution(1977542319875313158)
XLA Ops:
  0.6 49.8 %shard_map.155 = (bf16[128,16,128]{2,1,0:T(8,128)(2,1)}, f32[128,1,128]{2,1,0:T(1,128)}) custom-call(bf16[128,512]{1,0:T(8,128)(2,1)} %bitcast.7, bf16[128,512]{1,0:T(8,128)(2,1)} %bitcast.8, bf16[128,512]{1,0:T(8,128)(2,1)} %bitcast.9, bf16[128,512]{1,0:T(8,128)(2,1)} %bitcast.10, f32[128,512]{1,0:T(8,128)} %filt_hbm.1, f32[3,3,512]{2,1,0:T(4,128)} %taps_hbm.1, ...), custom_call_target="tpu_custom_call" | custom-call | tf_op jit(solution)/shard_map/pallas_call | solution.py:484
  50.4 3.4 %shard_map.156 = (bf16[128,512]{1,0:T(8,128)(2,1)}, bf16[128,512]{1,0:T(8,128)(2,1)}, bf16[128,512]{1,0:T(8,128)(2,1)}, f32[3,3,512]{2,1,0:T(4,128)}, f32[128,512]{1,0:T(8,128)}) custom-call(bf16[128,16,128]{2,1,0:T(8,128)(2,1)} %get-tuple-element.12.rows_hbm, f32[128,1,128]{2,1,0:T(1,128)} %get-tuple-element.13.taps_hbm, ...), custom_call_target="tpu_custom_call" | custom-call | tf_op jit(solution)/shard_map/pallas_call | solution.py:493

commit v3 on v2

--- a/solution.py
+++ b/solution.py
@@ -1,5 +1,4 @@
 import functools
-import itertools
 import math
 
 import jax
@@ -19,17 +18,9 @@
 CHAN = 4
 SEQ = 2
 POS = 128
-ROWS = 16
-REACH = 8
-
-
-def shell(reach):
-    hops = lambda d, n: min(d, n - d)
-    by_z = [
-        [(dx, dy, dz) for dy in range(4) for dx in range(4) if hops(dx, 4) + hops(dy, 4) + hops(dz, NZ) == reach]
-        for dz in (4, 3, 5, 2, 6, 1, 7, 0)
-    ]
-    return [d for row in itertools.zip_longest(*by_z) for d in row if d]
+PARTS = 2
+PAIR = CHAN // PARTS
+ROWS = 4 * PAIR
 
 
 def split_np(table):
@@ -57,13 +48,16 @@
     forward = np.stack(split_np(np.block([[c, -s], [s, c]])))
     inverse = np.stack(split_np(np.block([[c, s], [-s, c]])))
     twiddle = np.stack([np.cos(turn), np.sin(turn)]).astype(np.float32)
-    pick = np.zeros((32, 4, CHAN, 4, POS), np.float32)
+    pick = np.zeros((PARTS, 32, 4, PAIR, 4, POS), np.float32)
+    pick_one = np.zeros((32, 8, POS), np.float32)
     for g in range(32):
-        for f in range(4):
-            for i in range(CHAN):
-                pick[g, f, i, f, CHAN * g + i] = 1
+        for i in range(CHAN):
+            pick_one[g, i, CHAN * g + i] = 1
+            for f in range(4):
+                pick[i // PAIR, g, f, i % PAIR, f, CHAN * g + i] = 1
     pick = pick.reshape(512, 512).astype(jnp.bfloat16)
-    return first_cat, last_cat, forward, inverse, twiddle, pick
+    pick_one = pick_one.reshape(256, POS).astype(jnp.bfloat16)
+    return first_cat, last_cat, forward, inverse, twiddle, pick_one, pick
 
 
 def split(x):
@@ -94,9 +88,9 @@
 
 
 def kernel(
-    q_hbm, k_hbm, v_hbm, c_hbm, filt_hbm, taps_hbm, first_hbm, last_hbm, fwd_hbm, inv_hbm, tw_hbm, pick_hbm,
+    q_hbm, k_hbm, v_hbm, c_hbm, filt_hbm, taps_hbm, first_hbm, last_hbm, fwd_hbm, inv_hbm, tw_hbm, pick1_hbm, pick_hbm,
     rrecv, tap_recv,
-    q_ref, k_ref, v_ref, c_ref, filt_ref, taps_ref, first_ref, last_ref, fwd_ref, inv_ref, tw_ref, pick_ref,
+    q_ref, k_ref, v_ref, c_ref, filt_ref, taps_ref, first_ref, last_ref, fwd_ref, inv_ref, tw_ref, pick1_ref, pick_ref,
     send_buf, recv_buf, fsend, frecv, raw, fraw, spec, hspec, keep, pack, rsend,
     sib_send, sib_recv, tap_rows, tap_own, tap_sib, tap_send,
     load_sems, send_sem, recv_sem, fsend_sem, frecv_sem, rsend_sem, rrecv_sem,
@@ -108,33 +102,6 @@
     z = zh * 4 + zl
     me = zh * NCTX + cx
 
-    def place(zt, yt, xt, core_t):
-        half = zt // 4
-        ctx = yt * 16 + (zt - 4 * half) * 4 + xt
-        return (half * 2 + core_t, ctx), half * NCTX + ctx
-
-    def over(planes, act):
-        bases = []
-        for zt, own in planes:
-            half = zt // 4
-            bases.append((half * 2 + core, (zt - 4 * half) * 4, half * NCTX, own))
-
-        def row(dy, carry, skip=False):
-            yt = wrap(y + dy, 4) * 16
-            for dx in (2, 1, 3, 0):
-                for n, (dp_t, zrow, owner, own) in enumerate(bases):
-                    if own and skip and dx == 0:
-                        continue
-                    ctx = yt + zrow + xs[dx]
-                    act(n, (dp_t, ctx), owner + ctx)
-            return carry
-
-        if any(own for _, own in planes):
-            row(0, 0, True)
-            lax.fori_loop(1, 4, row, 0)
-        else:
-            lax.fori_loop(0, 4, row, 0)
-
     def plane_of(k):
         return wrap(z + k, NZ)
 
@@ -171,7 +138,7 @@
         pltpu.make_async_copy(source, target, load_sems.at[n])
         for n, (source, target) in enumerate([
             (pick_hbm, pick_ref), (q_hbm, q_ref), (k_hbm, k_ref), (v_hbm, v_ref), (c_hbm, c_ref),
-            (filt_hbm, filt_ref), (first_hbm, first_ref), (fwd_hbm, fwd_ref), (tw_hbm, tw_ref),
+            (filt_hbm, filt_ref), (pick1_hbm, pick1_ref), (first_hbm, first_ref), (fwd_hbm, fwd_ref), (tw_hbm, tw_ref),
             (taps_hbm, taps_ref), (inv_hbm, inv_ref), (last_hbm, last_ref),
         ])
     ]
@@ -184,15 +151,16 @@
         lanes = slice(j * POS, (j + 1) * POS)
         fields = jnp.concatenate([q_ref[:, lanes], k_ref[:, lanes], v_ref[:, lanes], c_ref[:, lanes]], axis=1)
         rows = dot_nt(pick_ref[...], fields).astype(BF16)
-        send_buf[pl.ds(j * 32, 32)] = rows.reshape(32, ROWS, POS)
+        send_buf[:, pl.ds(j * 32, 32)] = rows.reshape(PARTS, 32, ROWS, POS)
     loads[5].wait()
+    loads[6].wait()
     for j in range(4):
         lanes = slice(j * POS, (j + 1) * POS)
-        rows = dot_nt(pick_ref[:, :POS], filt_ref[:, lanes].astype(BF16)).astype(BF16)
-        fsend[pl.ds(j * 32, 32)] = rows.reshape(32, ROWS, POS)[:, :CHAN, :]
-
-    own = pltpu.make_async_copy(send_buf.at[me], recv_buf.at[me], recv_sem.at[zh])
-    own.start()
+        rows = dot_nt(pick1_ref[...], filt_ref[:, lanes].astype(BF16))
+        fsend[pl.ds(j * 32, 32)] = rows.reshape(32, 8, POS)[:, :CHAN, :].astype(BF16)
+
+    for part in range(PARTS):
+        pltpu.make_async_copy(send_buf.at[part, me], recv_buf.at[part, me], recv_sem.at[part]).start()
     fown = pltpu.make_async_copy(fsend.at[me], frecv.at[cx], frecv_sem)
     fown.start()
 
@@ -200,17 +168,20 @@
     for dz in (4, 3, 5, 2, 6, 1, 7):
         signal_to(columns[dz], plane_sem.at[NZ - dz])
     near = (0, 1, 2, 7)
-    plane = [(dx, dy) for dy in (2, 1, 3, 0) for dx in (2, 1, 3, 0)]
+    others = [
+        (dx, dy, dz)
+        for dy in (2, 1, 3, 0) for dx in (2, 1, 3, 0) for dz in (4, 3, 5, 2, 6, 1, 7, 0) if dx or dy or dz
+    ]
     for dz in range(1, NZ):
         pl.semaphore_wait(plane_sem.at[dz], 1)
-    for dx, dy in plane:
-        for d in [(dx, dy, dz) for dz in (4, 3, 5, 2, 6, 1, 7, 0) if dx or dy or dz]:
+    for part in range(PARTS):
+        for d in others:
             to, owner = target(*d)
             pltpu.make_async_remote_copy(
-                src_ref=send_buf.at[owner], dst_ref=recv_buf.at[me], send_sem=send_sem, recv_sem=recv_sem.at[zh],
-                device_id=to, device_id_type=MESH,
+                src_ref=send_buf.at[part, owner], dst_ref=recv_buf.at[part, me],
+                send_sem=send_sem.at[part], recv_sem=recv_sem.at[part], device_id=to, device_id_type=MESH,
             ).start()
-            if d[2] in near:
+            if part == 0 and d[2] in near:
                 pltpu.make_async_remote_copy(
                     src_ref=fsend.at[owner], dst_ref=frecv.at[cx], send_sem=fsend_sem, recv_sem=frecv_sem,
                     device_id=to, device_id_type=MESH,
@@ -232,7 +203,7 @@
         carried = jnp.where(row_id == NCTX - 1, 0.0, pltpu.roll(turned, NCTX - 1, 0))
         return jnp.where(lane_id >= POS - s, carried, turned)
 
-    for load in loads[6:]:
+    for load in loads[7:]:
         load.wait()
     channel = lax.broadcasted_iota(jnp.int32, (3, GROUP * CHAN), 1)
     tap_values = [
@@ -244,7 +215,7 @@
         return tap_values[branch][i][j:j + 1]
 
     def field(h, f, i):
-        return raw[h, pl.ds(f * CHAN + i, NCTX, ROWS), :]
+        return raw[pl.ds(h * NCTX * ROWS + f * PAIR + i, NCTX, ROWS), :]
 
     cos, sin = tw_ref[0], tw_ref[1]
 
@@ -273,83 +244,86 @@
     fraw[...] = jnp.concatenate([filt, jnp.zeros_like(filt)], axis=1).reshape(NCTX * 8, POS)
     hspec[...] = spectrum([fraw[pl.ds(i, NCTX, 8), :] for i in range(CHAN)])
 
-    for h in (zh, 1 - zh):
-        wait_bytes(recv_buf.at[pl.ds(h * NCTX, NCTX)], recv_sem.at[h])
-        raw[h] = recv_buf[pl.ds(h * NCTX, NCTX)].astype(F32).reshape(NCTX * ROWS, POS)
+    tap_rows[...] = jnp.zeros_like(tap_rows)
+    pairs = [(h, i) for h in range(SEQ) for i in range(PAIR)]
+    for part in range(PARTS):
+        wait_bytes(recv_buf.at[part], recv_sem.at[part])
+        raw[...] = recv_buf[part].astype(F32).reshape(GROUP * ROWS, POS)
         values = []
-        for i in range(CHAN):
+        for n, (h, i) in enumerate(pairs):
             feats = []
             for branch in range(3):
                 v = field(h, branch, i)
+                c = part * PAIR + i
                 feats.append(
-                    tap(branch, 0, i) * v + tap(branch, 1, i) * before(v, 1) + tap(branch, 2, i) * before(v, 2)
+                    tap(branch, 0, c) * v + tap(branch, 1, c) * before(v, 1) + tap(branch, 2, c) * before(v, 2)
                 )
-            keep[h, i, 0] = feats[1]
-            keep[h, i, 1] = feats[2]
+            keep[n, 0] = feats[1]
+            keep[n, 1] = feats[2]
             values += [feats[1] * feats[2], feats[0] * field(h, 3, i)]
-        spec[h] = spectrum(values)
-
-    corrs = []
-    for i in range(CHAN):
-        re = im = 0.0
-        for h in range(SEQ):
-            mr, mi = halves(spec.at[h], 2 * i)
-            gr, gi = halves(spec.at[h], 2 * i + 1)
-            re, im = re + (mr * gr + mi * gi), im + (mr * gi - mi * gr)
-        corrs.append((re, im))
-    sib_send[...] = signal(corrs)
-    sib = pltpu.make_async_remote_copy(
-        src_ref=sib_send, dst_ref=sib_recv, send_sem=sib_sems.at[0], recv_sem=sib_sems.at[1],
-        device_id=sibling, device_id_type=MESH,
-    )
-    sib.start()
-
-    tap_rows[...] = jnp.zeros_like(tap_rows)
-    for step, h in enumerate((1 - zh, zh)):
+        spec[...] = spectrum(values)
+
+        corrs = []
+        for i in range(PAIR):
+            re = im = 0.0
+            for h in range(SEQ):
+                n = h * PAIR + i
+                mr, mi = halves(spec, 2 * n)
+                gr, gi = halves(spec, 2 * n + 1)
+                re, im = re + (mr * gr + mi * gi), im + (mr * gi - mi * gr)
+            corrs.append((re, im))
+        sib_send[part] = signal(corrs)
+        sib = pltpu.make_async_remote_copy(
+            src_ref=sib_send.at[part], dst_ref=sib_recv.at[part],
+            send_sem=sib_sems.at[0, part], recv_sem=sib_sems.at[1, part], device_id=sibling, device_id_type=MESH,
+        )
+        sib.start()
+
         spectra = []
-        for i in range(CHAN):
-            fr, fi = halves(hspec, i)
-            mr, mi = halves(spec.at[h], 2 * i)
-            gr, gi = halves(spec.at[h], 2 * i + 1)
+        for n, (h, i) in enumerate(pairs):
+            fr, fi = halves(hspec, part * PAIR + i)
+            mr, mi = halves(spec, 2 * n)
+            gr, gi = halves(spec, 2 * n + 1)
             spectra += [(fr * mr - fi * mi, fr * mi + fi * mr), (fr * gr + fi * gi, fr * gi - fi * gr)]
         back = signal(spectra)
         grads = []
-        for i in range(CHAN):
-            conv = back[:, 2 * i * POS:(2 * i + 1) * POS]
-            adj = back[:, (2 * i + 1) * POS:(2 * i + 2) * POS]
-            grads.append([field(h, 3, i) * conv, adj * keep[h, i, 1], adj * keep[h, i, 0]])
+        for n, (h, i) in enumerate(pairs):
+            conv = back[:, 2 * n * POS:(2 * n + 1) * POS]
+            adj = back[:, (2 * n + 1) * POS:(2 * n + 2) * POS]
+            grads.append([field(h, 3, i) * conv, adj * keep[n, 1], adj * keep[n, 0]])
+            c = part * PAIR + i
             for branch in range(3):
-                d = grads[i][branch]
-                pack[pl.ds(branch * CHAN + i, NCTX, ROWS), :] = (
-                    tap(branch, 0, i) * d + tap(branch, 1, i) * after(d, 1) + tap(branch, 2, i) * after(d, 2)
+                d = grads[n][branch]
+                pack[pl.ds(h * NCTX * ROWS + branch * PAIR + i, NCTX, ROWS), :] = (
+                    tap(branch, 0, c) * d + tap(branch, 1, c) * after(d, 1) + tap(branch, 2, c) * after(d, 2)
                 )
-        if step == 0:
-            sib.wait_recv()
-            for i in range(CHAN):
-                pack[pl.ds(3 * CHAN + i, NCTX, ROWS), :] = (
-                    sib_send[:, i * POS:(i + 1) * POS] + sib_recv[:, i * POS:(i + 1) * POS]
-                )
+
         def tap_terms():
-            for i in range(CHAN):
+            for n, (h, i) in enumerate(pairs):
                 for branch in range(3):
-                    d, v = grads[i][branch], field(h, branch, i)
+                    d, v = grads[n][branch], field(h, branch, i)
                     for j in range(3):
                         term = d * (before(v, j) if j else v)
-                        row = (branch * 3 + j) * CHAN + i
+                        row = (branch * 3 + j) * CHAN + part * PAIR + i
                         tap_rows[row:row + 1, :] += jnp.sum(term, axis=0, keepdims=True)
 
-        def give(n, to, owner):
-            pltpu.make_async_remote_copy(
-                src_ref=rsend.at[owner], dst_ref=rrecv.at[me], send_sem=rsend_sem, recv_sem=rrecv_sem,
-                device_id=to, device_id_type=MESH,
-            ).start()
-
-        def give_all():
-            rsend[pl.ds(h * NCTX, NCTX)] = pack[...].reshape(NCTX, ROWS, POS).astype(BF16)
-            over([(h * 4 + wrap(zl + t, 4), step == 1 and t == 0) for t in range(4)], give)
-
-        if step == 0:
-            give_all()
+        def give():
+            sib.wait()
+            for i in range(PAIR):
+                total = sib_send[part, :, i * POS:(i + 1) * POS] + sib_recv[part, :, i * POS:(i + 1) * POS]
+                for h in range(SEQ):
+                    pack[pl.ds(h * NCTX * ROWS + 3 * PAIR + i, NCTX, ROWS), :] = total
+            rsend[part] = pack[...].reshape(GROUP, ROWS, POS).astype(BF16)
+            for d in others:
+                to, owner = target(*d)
+                pltpu.make_async_remote_copy(
+                    src_ref=rsend.at[part, owner], dst_ref=rrecv.at[part, me],
+                    send_sem=rsend_sem.at[part], recv_sem=rrecv_sem.at[part], device_id=to, device_id_type=MESH,
+                ).start()
+            pltpu.make_async_copy(rsend.at[part, me], rrecv.at[part, me], rrecv_sem.at[part]).start()
+
+        if part < PARTS - 1:
+            give()
             tap_terms()
         else:
             tap_terms()
@@ -362,31 +336,25 @@
                 device_id=sibling, device_id_type=MESH,
             )
             tap_sibling.start()
-            give_all()
-    tap_sibling.wait_recv()
+            give()
+    tap_sibling.wait()
     tap_send[...] = tap_own[...] + tap_sib[...]
-    for dy in (2, 1, 3, 0):
-        for dx in (2, 1, 3, 0):
-            for dz in (4, 3, 5, 2, 6, 1, 7, 0):
-                if dx or dy or dz:
-                    pltpu.make_async_remote_copy(
-                        src_ref=tap_send, dst_ref=tap_recv.at[me], send_sem=tap_sems.at[2], recv_sem=tap_sems.at[3],
-                        device_id=target(dx, dy, dz)[0], device_id_type=MESH,
-                    ).start()
-    town = pltpu.make_async_copy(tap_send, tap_recv.at[me], tap_sems.at[3])
-    town.start()
-    rown = pltpu.make_async_copy(rsend.at[me], rrecv.at[me], rrecv_sem)
-    rown.start()
-
-    wait_bytes(send_buf.at[pl.ds(0, GROUP - 1)], send_sem)
+    for d in others:
+        pltpu.make_async_remote_copy(
+            src_ref=tap_send, dst_ref=tap_recv.at[me], send_sem=tap_sems.at[2], recv_sem=tap_sems.at[3],
+            device_id=target(*d)[0], device_id_type=MESH,
+        ).start()
+    pltpu.make_async_copy(tap_send, tap_recv.at[me], tap_sems.at[3]).start()
+
     wait_bytes(fsend.at[pl.ds(0, NCTX - 1)], fsend_sem)
-    sib.wait_send()
-    tap_sibling.wait_send()
-
-    wait_bytes(rrecv, rrecv_sem)
+    for part in range(PARTS):
+        wait_bytes(send_buf.at[part, pl.ds(0, GROUP - 1)], send_sem.at[part])
+    for part in range(PARTS):
+        wait_bytes(rsend.at[part, pl.ds(0, GROUP - 1)], rsend_sem.at[part])
+    wait_bytes(tap_recv.at[pl.ds(0, GROUP - 1)], tap_sems.at[2])
+    for part in range(PARTS):
+        wait_bytes(rrecv.at[part], rrecv_sem.at[part])
     wait_bytes(tap_recv, tap_sems.at[3])
-    wait_bytes(rsend.at[pl.ds(0, GROUP - 1)], rsend_sem)
-    wait_bytes(tap_recv.at[pl.ds(0, GROUP - 1)], tap_sems.at[2])
 
 
 def finish(
@@ -396,7 +364,7 @@
     load_pick = pltpu.make_async_copy(pick_hbm, pick_ref, load_sems.at[0])
     load_pick.start()
     loads = [
-        pltpu.make_async_copy(rows_hbm.at[pl.ds(j * 32, 32)], rows_ref.at[pl.ds(j * 32, 32)], load_sems.at[1 + j])
+        pltpu.make_async_copy(rows_hbm.at[:, pl.ds(j * 32, 32)], rows_ref.at[:, pl.ds(j * 32, 32)], load_sems.at[1 + j])
         for j in range(4)
     ]
     for load in loads:
@@ -414,7 +382,7 @@
     for j in range(4):
         lanes = pl.ds(j * POS, POS)
         loads[j].wait()
-        rows = rows_ref[pl.ds(j * 32, 32)].reshape(512, POS)
+        rows = rows_ref[:, pl.ds(j * 32, 32)].reshape(512, POS)
         out = lax.dot_general(rows, pick_ref[...], (((0,), (0,)), ((), ())), preferred_element_type=F32)
         gq_ref[:, lanes] = out[:, :POS].astype(BF16)
         gk_ref[:, lanes] = out[:, POS:2 * POS].astype(BF16)
@@ -452,38 +420,38 @@
     constants = [jnp.asarray(t) for t in tables()]
     operands = [query_in[0], key_in[0], value_in[0], cotangent[0], long_filter, short_taps, *constants]
     scratch = [pltpu.VMEM(v.shape, v.dtype) for v in operands] + [
-        pltpu.VMEM((GROUP, ROWS, POS), BF16),
-        pltpu.VMEM((GROUP, ROWS, POS), BF16),
+        pltpu.VMEM((PARTS, GROUP, ROWS, POS), BF16),
+        pltpu.VMEM((PARTS, GROUP, ROWS, POS), BF16),
         pltpu.VMEM((GROUP, CHAN, POS), BF16),
         pltpu.VMEM((NCTX, CHAN, POS), BF16),
-        pltpu.VMEM((SEQ, NCTX * ROWS, POS), F32),
+        pltpu.VMEM((GROUP * ROWS, POS), F32),
         pltpu.VMEM((NCTX * 8, POS), F32),
-        pltpu.VMEM((SEQ, 2 * CHAN * NCTX, 2 * POS), F32),
+        pltpu.VMEM((2 * SEQ * PAIR * NCTX, 2 * POS), F32),
         pltpu.VMEM((CHAN * NCTX, 2 * POS), F32),
-        pltpu.VMEM((SEQ, CHAN, 2, NCTX, POS), F32),
-        pltpu.VMEM((NCTX * ROWS, POS), F32),
-        pltpu.VMEM((GROUP, ROWS, POS), BF16),
-        pltpu.VMEM((NCTX, CHAN * POS), F32),
-        pltpu.VMEM((NCTX, CHAN * POS), F32),
+        pltpu.VMEM((SEQ * PAIR, 2, NCTX, POS), F32),
+        pltpu.VMEM((GROUP * ROWS, POS), F32),
+        pltpu.VMEM((PARTS, GROUP, ROWS, POS), BF16),
+        pltpu.VMEM((PARTS, NCTX, PAIR * POS), F32),
+        pltpu.VMEM((PARTS, NCTX, PAIR * POS), F32),
         pltpu.VMEM((POS, POS), F32),
         pltpu.VMEM((1, POS), F32),
         pltpu.VMEM((1, POS), F32),
         pltpu.VMEM((1, POS), F32),
         pltpu.SemaphoreType.DMA((len(operands),)),
-        pltpu.SemaphoreType.DMA,
-        pltpu.SemaphoreType.DMA((SEQ,)),
+        pltpu.SemaphoreType.DMA((PARTS,)),
+        pltpu.SemaphoreType.DMA((PARTS,)),
         pltpu.SemaphoreType.DMA,
         pltpu.SemaphoreType.DMA,
-        pltpu.SemaphoreType.DMA,
-        pltpu.SemaphoreType.DMA,
-        pltpu.SemaphoreType.DMA((2,)),
+        pltpu.SemaphoreType.DMA((PARTS,)),
+        pltpu.SemaphoreType.DMA((PARTS,)),
+        pltpu.SemaphoreType.DMA((2, PARTS)),
         pltpu.SemaphoreType.DMA((4,)),
         pltpu.SemaphoreType.REGULAR((NZ,)),
     ]
     params = functools.partial(pltpu.CompilerParams, vmem_limit_bytes=63 * 1024 * 1024)
     held = pl.pallas_call(
         kernel,
-        out_shape=(shape((GROUP, ROWS, POS), BF16), shape((GROUP, 1, POS), F32)),
+        out_shape=(shape((PARTS, GROUP, ROWS, POS), BF16), shape((GROUP, 1, POS), F32)),
         in_specs=[hbm] * len(operands),
         out_specs=[hbm] * 2,
         scratch_shapes=scratch,

time: 54 us -> 48.9 us (0.906)
  Pallas kernels: 53.2 us -> 48.1 us
    pallas_call x1, Pallas kernels: 49.8 us -> 44.7 us  [per_device(): pl.pallas_call(kernel, out_shape=(shape((PARTS, GROUP, ROWS, POS), BF16),...]
where the time goes in v3:
time: 48.9 us; the launch traced here: 48.8 us
  Pallas kernels  48.1 us (98%)
  between operations  0.64 us (1%)
    pallas_call x1, Pallas kernels, per_device(): pl.pallas_call(kernel, out_shape=(shape((PARTS, GROUP, ROWS, POS), BF16),...  44.7 us
    pallas_call x1, Pallas kernels, per_device(): pl.pallas_call(finish, out_shape=results, in_specs=[hbm] * 3, out_specs=[...  3.41 us

profile of v3, /device:TPU:1, one launch (start us, length us, event | category | flops | bytes accessed | tf_op | source)
XLA Modules:
  0.0 48.8 jit_solution(375130115963483063)
XLA Ops:
  0.6 44.7 %shard_map.164 = (bf16[2,128,8,128]{3,2,1,0:T(8,128)(2,1)}, f32[128,1,128]{2,1,0:T(1,128)}) custom-call(bf16[128,512]{1,0:T(8,128)(2,1)} %bitcast.7, bf16[128,512]{1,0:T(8,128)(2,1)} %bitcast.8, bf16[128,512]{1,0:T(8,128)(2,1)} %bitcast.9, bf16[128,512]{1,0:T(8,128)(2,1)} %bitcast.10, f32[128,512]{1,0:T(8,128)} %filt_hbm.1, f32[3,3,512]{2,1,0:T(4,128)} %taps_hbm.1, ...), custom_call_target="tpu_custom_call" | custom-call | tf_op jit(solution)/shard_map/pallas_call | solution.py:452
  45.4 3.4 %shard_map.165 = (bf16[128,512]{1,0:T(8,128)(2,1)}, bf16[128,512]{1,0:T(8,128)(2,1)}, bf16[128,512]{1,0:T(8,128)(2,1)}, f32[3,3,512]{2,1,0:T(4,128)}, f32[128,512]{1,0:T(8,128)}) custom-call(bf16[2,128,8,128]{3,2,1,0:T(8,128)(2,1)} %get-tuple-element.12.rows_hbm, f32[128,1,128]{2,1,0:T(1,128)} %get-tuple-element.13.taps_hbm, ...), custom_call_target="tpu_custom_call" | custom-call | tf_op jit(solution)/shard_map/pallas_call | solution.py:461

commit v4 on v3

--- a/solution.py
+++ b/solution.py
@@ -18,9 +18,10 @@
 CHAN = 4
 SEQ = 2
 POS = 128
-PARTS = 2
+PARTS = 4
 PAIR = CHAN // PARTS
 ROWS = 4 * PAIR
+HELD = 8
 
 
 def split_np(table):
@@ -55,9 +56,13 @@
             pick_one[g, i, CHAN * g + i] = 1
             for f in range(4):
                 pick[i // PAIR, g, f, i % PAIR, f, CHAN * g + i] = 1
+    back = pick.copy()
+    back[:, :, 3] = 0
+    back[1:, :, 3] = pick[:-1, :, 3]
+    back = np.concatenate([back.reshape(512, 512), pick[-1, :, 3].reshape(32, 512)]).astype(jnp.bfloat16)
     pick = pick.reshape(512, 512).astype(jnp.bfloat16)
     pick_one = pick_one.reshape(256, POS).astype(jnp.bfloat16)
-    return first_cat, last_cat, forward, inverse, twiddle, pick_one, pick
+    return (first_cat, last_cat, forward, inverse, twiddle, pick_one, pick), back
 
 
 def split(x):
@@ -125,13 +130,12 @@
         ctx = ys[dy] + zrow + xs[dx]
         return (dp_t, ctx), first + ctx
 
-    columns = [target(0, 0, dz)[0] for dz in range(NZ)]
-    for dz in (4, 3, 5, 2, 6, 1, 7):
-        signal_to(columns[dz], barrier)
-    for dy in (2, 1, 3, 0):
-        for dx in (2, 1, 3, 0):
-            if dx or dy:
-                signal_to(target(dx, dy, 0)[0], barrier)
+    others = [
+        (dx, dy, dz)
+        for dz in (4, 3, 5, 2, 6, 1, 7, 0) for dy in (2, 1, 3, 0) for dx in (2, 1, 3, 0) if dx or dy or dz
+    ]
+    for d in others:
+        signal_to(target(*d)[0], barrier)
     signal_to(sibling, barrier)
 
     loads = [
@@ -164,16 +168,12 @@
     fown = pltpu.make_async_copy(fsend.at[me], frecv.at[cx], frecv_sem)
     fown.start()
 
-    pl.semaphore_wait(barrier, NPLANE - 1 + NZ - 1 + 1)
-    for dz in (4, 3, 5, 2, 6, 1, 7):
-        signal_to(columns[dz], plane_sem.at[NZ - dz])
+    pl.semaphore_wait(barrier, GROUP)
     near = (0, 1, 2, 7)
     others = [
         (dx, dy, dz)
         for dy in (2, 1, 3, 0) for dx in (2, 1, 3, 0) for dz in (4, 3, 5, 2, 6, 1, 7, 0) if dx or dy or dz
     ]
-    for dz in range(1, NZ):
-        pl.semaphore_wait(plane_sem.at[dz], 1)
     for part in range(PARTS):
         for d in others:
             to, owner = target(*d)
@@ -215,7 +215,7 @@
         return tap_values[branch][i][j:j + 1]
 
     def field(h, f, i):
-        return raw[pl.ds(h * NCTX * ROWS + f * PAIR + i, NCTX, ROWS), :]
+        return raw[pl.ds(h * NCTX * HELD + f * PAIR + i, NCTX, HELD), :]
 
     cos, sin = tw_ref[0], tw_ref[1]
 
@@ -246,9 +246,22 @@
 
     tap_rows[...] = jnp.zeros_like(tap_rows)
     pairs = [(h, i) for h in range(SEQ) for i in range(PAIR)]
+    sibs = []
+
+    def filter_total(part):
+        sibs[part].wait()
+        return sib_send[part] + sib_recv[part]
+
+    def filter_rows(part):
+        total = filter_total(part)
+        for h in range(SEQ):
+            pack[pl.ds(h * NCTX * HELD + 3, NCTX, HELD), :] = total
+
+    pack[...] = jnp.zeros_like(pack)
     for part in range(PARTS):
         wait_bytes(recv_buf.at[part], recv_sem.at[part])
-        raw[...] = recv_buf[part].astype(F32).reshape(GROUP * ROWS, POS)
+        arrived = recv_buf[part].astype(F32)
+        raw[...] = jnp.concatenate([arrived, jnp.zeros_like(arrived)], axis=1).reshape(GROUP * HELD, POS)
         values = []
         for n, (h, i) in enumerate(pairs):
             feats = []
@@ -278,6 +291,7 @@
             send_sem=sib_sems.at[0, part], recv_sem=sib_sems.at[1, part], device_id=sibling, device_id_type=MESH,
         )
         sib.start()
+        sibs.append(sib)
 
         spectra = []
         for n, (h, i) in enumerate(pairs):
@@ -294,7 +308,7 @@
             c = part * PAIR + i
             for branch in range(3):
                 d = grads[n][branch]
-                pack[pl.ds(h * NCTX * ROWS + branch * PAIR + i, NCTX, ROWS), :] = (
+                pack[pl.ds(h * NCTX * HELD + branch * PAIR + i, NCTX, HELD), :] = (
                     tap(branch, 0, c) * d + tap(branch, 1, c) * after(d, 1) + tap(branch, 2, c) * after(d, 2)
                 )
 
@@ -308,12 +322,9 @@
                         tap_rows[row:row + 1, :] += jnp.sum(term, axis=0, keepdims=True)
 
         def give():
-            sib.wait()
-            for i in range(PAIR):
-                total = sib_send[part, :, i * POS:(i + 1) * POS] + sib_recv[part, :, i * POS:(i + 1) * POS]
-                for h in range(SEQ):
-                    pack[pl.ds(h * NCTX * ROWS + 3 * PAIR + i, NCTX, ROWS), :] = total
-            rsend[part] = pack[...].reshape(GROUP, ROWS, POS).astype(BF16)
+            if part:
+                filter_rows(part - 1)
+            rsend[part] = pack[...].reshape(GROUP, HELD, POS)[:, :ROWS, :].astype(BF16)
             for d in others:
                 to, owner = target(*d)
                 pltpu.make_async_remote_copy(
@@ -338,13 +349,17 @@
             tap_sibling.start()
             give()
     tap_sibling.wait()
-    tap_send[...] = tap_own[...] + tap_sib[...]
+    total = filter_total(PARTS - 1).reshape(NCTX, 1, POS)
+    for h in range(SEQ):
+        tap_send[pl.ds(h * NCTX, NCTX), 0:1, :] = total
+    tap_send[:, 1:2, :] = jnp.broadcast_to((tap_own[...] + tap_sib[...]).reshape(1, 1, POS), (GROUP, 1, POS))
     for d in others:
+        to, owner = target(*d)
         pltpu.make_async_remote_copy(
-            src_ref=tap_send, dst_ref=tap_recv.at[me], send_sem=tap_sems.at[2], recv_sem=tap_sems.at[3],
-            device_id=target(*d)[0], device_id_type=MESH,
+            src_ref=tap_send.at[owner], dst_ref=tap_recv.at[me], send_sem=tap_sems.at[2], recv_sem=tap_sems.at[3],
+            device_id=to, device_id_type=MESH,
         ).start()
-    pltpu.make_async_copy(tap_send, tap_recv.at[me], tap_sems.at[3]).start()
+    pltpu.make_async_copy(tap_send.at[me], tap_recv.at[me], tap_sems.at[3]).start()
 
     wait_bytes(fsend.at[pl.ds(0, NCTX - 1)], fsend_sem)
     for part in range(PARTS):
@@ -378,11 +393,15 @@
     lane = lax.broadcasted_iota(jnp.int32, (CHAN * GROUP, GROUP * CHAN), 1)
     spread = (lane == CHAN * (row % GROUP) + row // GROUP).astype(F32).astype(BF16)
     load_pick.wait()
+    load_taps.wait()
     outs = []
     for j in range(4):
         lanes = pl.ds(j * POS, POS)
         loads[j].wait()
-        rows = rows_ref[:, pl.ds(j * 32, 32)].reshape(512, POS)
+        rows = jnp.concatenate([
+            rows_ref[:, pl.ds(j * 32, 32)].reshape(512, POS),
+            taps_ref[pl.ds(j * 32, 32), 0, :].astype(BF16),
+        ], axis=0)
         out = lax.dot_general(rows, pick_ref[...], (((0,), (0,)), ((), ())), preferred_element_type=F32)
         gq_ref[:, lanes] = out[:, :POS].astype(BF16)
         gk_ref[:, lanes] = out[:, POS:2 * POS].astype(BF16)
@@ -392,8 +411,7 @@
             outs.append(pltpu.make_async_copy(source.at[:, lanes], target.at[:, lanes], out_sems.at[4 * j + n]))
             outs[-1].start()
 
-    load_taps.wait()
-    high, low = split(taps_ref[...].reshape(GROUP, POS))
+    high, low = split(taps_ref[:, 1, :])
     rows = dot_nt(pick_row, high) + dot_nt(pick_row, low)
     high, low = split(jnp.concatenate([rows[i * 16:(i + 1) * 16] for i in range(CHAN)], axis=1))
     both = dot(jnp.concatenate([high, low], axis=0), spread)
@@ -417,26 +435,27 @@
         shape(short_taps.shape, F32),
         shape((rows, channels), F32),
     )
-    constants = [jnp.asarray(t) for t in tables()]
+    constants, back = tables()
+    constants = [jnp.asarray(t) for t in constants]
     operands = [query_in[0], key_in[0], value_in[0], cotangent[0], long_filter, short_taps, *constants]
     scratch = [pltpu.VMEM(v.shape, v.dtype) for v in operands] + [
         pltpu.VMEM((PARTS, GROUP, ROWS, POS), BF16),
         pltpu.VMEM((PARTS, GROUP, ROWS, POS), BF16),
         pltpu.VMEM((GROUP, CHAN, POS), BF16),
         pltpu.VMEM((NCTX, CHAN, POS), BF16),
-        pltpu.VMEM((GROUP * ROWS, POS), F32),
+        pltpu.VMEM((GROUP * HELD, POS), F32),
         pltpu.VMEM((NCTX * 8, POS), F32),
         pltpu.VMEM((2 * SEQ * PAIR * NCTX, 2 * POS), F32),
         pltpu.VMEM((CHAN * NCTX, 2 * POS), F32),
         pltpu.VMEM((SEQ * PAIR, 2, NCTX, POS), F32),
-        pltpu.VMEM((GROUP * ROWS, POS), F32),
+        pltpu.VMEM((GROUP * HELD, POS), F32),
         pltpu.VMEM((PARTS, GROUP, ROWS, POS), BF16),
         pltpu.VMEM((PARTS, NCTX, PAIR * POS), F32),
         pltpu.VMEM((PARTS, NCTX, PAIR * POS), F32),
         pltpu.VMEM((POS, POS), F32),
         pltpu.VMEM((1, POS), F32),
         pltpu.VMEM((1, POS), F32),
-        pltpu.VMEM((1, POS), F32),
+        pltpu.VMEM((GROUP, 2, POS), F32),
         pltpu.SemaphoreType.DMA((len(operands),)),
         pltpu.SemaphoreType.DMA((PARTS,)),
         pltpu.SemaphoreType.DMA((PARTS,)),
@@ -451,13 +470,13 @@
     params = functools.partial(pltpu.CompilerParams, vmem_limit_bytes=63 * 1024 * 1024)
     held = pl.pallas_call(
         kernel,
-        out_shape=(shape((PARTS, GROUP, ROWS, POS), BF16), shape((GROUP, 1, POS), F32)),
+        out_shape=(shape((PARTS, GROUP, ROWS, POS), BF16), shape((GROUP, 2, POS), F32)),
         in_specs=[hbm] * len(operands),
         out_specs=[hbm] * 2,
         scratch_shapes=scratch,
         compiler_params=params(collective_id=0, has_side_effects=True),
     )(*operands)
-    inner = [*held, operands[-1]]
+    inner = [*held, jnp.asarray(back)]
     grad_query, grad_key, grad_value, grad_taps, grad_filter = pl.pallas_call(
         finish,
         out_shape=results,

time: 48.9 us -> 47 us (0.961)
  Pallas kernels: 48.1 us -> 46.1 us
    pallas_call x1, Pallas kernels: 44.7 us -> 42.5 us  [per_device(): pl.pallas_call(kernel, out_shape=(shape((PARTS, GROUP, ROWS, POS), BF16),...]
where the time goes in v4:
time: 47 us; the launch traced here: 46.9 us
  Pallas kernels  46.1 us (98%)
  between operations  0.8 us (2%)
    pallas_call x1, Pallas kernels, per_device(): pl.pallas_call(kernel, out_shape=(shape((PARTS, GROUP, ROWS, POS), BF16),...  42.5 us
    pallas_call x1, Pallas kernels, per_device(): pl.pallas_call(finish, out_shape=results, in_specs=[hbm] * 3, out_specs=[...  3.56 us

profile of v4, /device:TPU:1, one launch (start us, length us, event | category | flops | bytes accessed | tf_op | source)
XLA Modules:
  0.0 46.9 jit_solution(482793393755935911)
XLA Ops:
  0.6 42.5 %shard_map.173 = (bf16[4,128,4,128]{3,2,1,0:T(4,128)(2,1)}, f32[128,2,128]{2,1,0:T(2,128)}) custom-call(bf16[128,512]{1,0:T(8,128)(2,1)} %bitcast.7, bf16[128,512]{1,0:T(8,128)(2,1)} %bitcast.8, bf16[128,512]{1,0:T(8,128)(2,1)} %bitcast.9, bf16[128,512]{1,0:T(8,128)(2,1)} %bitcast.10, f32[128,512]{1,0:T(8,128)} %filt_hbm.1, f32[3,3,512]{2,1,0:T(4,128)} %taps_hbm.1, ...), custom_call_target="tpu_custom_call" | custom-call | tf_op jit(solution)/shard_map/pallas_call | solution.py:471
  43.1 3.6 %shard_map.174 = (bf16[128,512]{1,0:T(8,128)(2,1)}, bf16[128,512]{1,0:T(8,128)(2,1)}, bf16[128,512]{1,0:T(8,128)(2,1)}, f32[3,3,512]{2,1,0:T(4,128)}, f32[128,512]{1,0:T(8,128)}) custom-call(bf16[4,128,4,128]{3,2,1,0:T(4,128)(2,1)} %get-tuple-element.12.rows_hbm, f32[128,2,128]{2,1,0:T(2,128)} %get-tuple-element.13.taps_hbm, ...), custom_call_target="tpu_custom_call" | custom-call | tf_op jit(solution)/shard_map/pallas_call | solution.py:480

commit v5 on v4

--- a/solution.py
+++ b/solution.py
@@ -262,15 +262,14 @@
         wait_bytes(recv_buf.at[part], recv_sem.at[part])
         arrived = recv_buf[part].astype(F32)
         raw[...] = jnp.concatenate([arrived, jnp.zeros_like(arrived)], axis=1).reshape(GROUP * HELD, POS)
-        values = []
+        values, delayed = [], []
         for n, (h, i) in enumerate(pairs):
             feats = []
             for branch in range(3):
                 v = field(h, branch, i)
                 c = part * PAIR + i
-                feats.append(
-                    tap(branch, 0, c) * v + tap(branch, 1, c) * before(v, 1) + tap(branch, 2, c) * before(v, 2)
-                )
+                delayed.append((v, before(v, 1), before(v, 2)))
+                feats.append(sum(tap(branch, j, c) * delayed[-1][j] for j in range(3)))
             keep[n, 0] = feats[1]
             keep[n, 1] = feats[2]
             values += [feats[1] * feats[2], feats[0] * field(h, 3, i)]
@@ -315,9 +314,9 @@
         def tap_terms():
             for n, (h, i) in enumerate(pairs):
                 for branch in range(3):
-                    d, v = grads[n][branch], field(h, branch, i)
+                    d = grads[n][branch]
                     for j in range(3):
-                        term = d * (before(v, j) if j else v)
+                        term = d * delayed[n * 3 + branch][j]
                         row = (branch * 3 + j) * CHAN + part * PAIR + i
                         tap_rows[row:row + 1, :] += jnp.sum(term, axis=0, keepdims=True)
 

time: 47 us -> 46.5 us (0.989)
  Pallas kernels: 46.1 us -> 45.5 us
    pallas_call x1, Pallas kernels: 42.5 us -> 42 us  [per_device(): pl.pallas_call(kernel, out_shape=(shape((PARTS, GROUP, ROWS, POS), BF16),...]
where the time goes in v5:
time: 46.5 us; the launch traced here: 46.3 us
  Pallas kernels  45.5 us (98%)
  between operations  0.8 us (2%)
    pallas_call x1, Pallas kernels, per_device(): pl.pallas_call(kernel, out_shape=(shape((PARTS, GROUP, ROWS, POS), BF16),...  42 us
    pallas_call x1, Pallas kernels, per_device(): pl.pallas_call(finish, out_shape=results, in_specs=[hbm] * 3, out_specs=[...  3.55 us

profile of v5, /device:TPU:1, one launch (start us, length us, event | category | flops | bytes accessed | tf_op | source)
XLA Modules:
  0.0 46.3 jit_solution(5238326627903704659)
XLA Ops:
  0.6 42.0 %shard_map.173 = (bf16[4,128,4,128]{3,2,1,0:T(4,128)(2,1)}, f32[128,2,128]{2,1,0:T(2,128)}) custom-call(bf16[128,512]{1,0:T(8,128)(2,1)} %bitcast.7, bf16[128,512]{1,0:T(8,128)(2,1)} %bitcast.8, bf16[128,512]{1,0:T(8,128)(2,1)} %bitcast.9, bf16[128,512]{1,0:T(8,128)(2,1)} %bitcast.10, f32[128,512]{1,0:T(8,128)} %filt_hbm.1, f32[3,3,512]{2,1,0:T(4,128)} %taps_hbm.1, ...), custom_call_target="tpu_custom_call" | custom-call | tf_op jit(solution)/shard_map/pallas_call | solution.py:470
  42.6 3.6 %shard_map.174 = (bf16[128,512]{1,0:T(8,128)(2,1)}, bf16[128,512]{1,0:T(8,128)(2,1)}, bf16[128,512]{1,0:T(8,128)(2,1)}, f32[3,3,512]{2,1,0:T(4,128)}, f32[128,512]{1,0:T(8,128)}) custom-call(bf16[4,128,4,128]{3,2,1,0:T(4,128)(2,1)} %get-tuple-element.12.rows_hbm, f32[128,2,128]{2,1,0:T(2,128)} %get-tuple-element.13.taps_hbm, ...), custom_call_target="tpu_custom_call" | custom-call | tf_op jit(solution)/shard_map/pallas_call | solution.py:479
